TPU v7x, 32 devices: a whole 2x2x4 slice. The times are simulated.
32 devices in a mesh: dir: 2 (over core), batch: 8 (over z, y), unit: 2 (over x).
Axes of the slice: x: 2, y: 2, z: 4, core: 2. Of those that a mesh axis runs over, the one named last changes fastest.
Arguments:
- inputs: bfloat16 [256, 16, 512], P('batch'), may hold values from -6 to 6
- win_count: int32 [256], P('batch'), may hold values from 1 to 2, as said below
- last_live: int32 [256], P('batch'), may hold values from 1 to 8, as said below
- hidden_init: float32 [2, 256, 512], P('dir', 'batch'), may hold values from -3 to 3
- cell_init: float32 [2, 256, 4096], P('dir', 'batch', 'unit'), may hold values from -3 to 3
- w_input: bfloat16 [2, 512, 4, 4096], P('dir', None, None, 'unit'), may hold values from -0.25 to 0.25
- w_hidden: bfloat16 [2, 512, 4, 4096], P('dir', None, None, 'unit'), may hold values from -0.25 to 0.25
- gate_bias: float32 [2, 4, 4096], P('dir', None, 'unit'), may hold values from -3 to 3
- w_proj: bfloat16 [2, 4096, 512], P('dir', 'unit'), may hold values from -0.375 to 0.375
- out_grad: bfloat16 [2, 256, 16, 512], P('dir', 'batch'), may hold values from -6 to 6
Outputs:
- layer_out: bfloat16 [2, 256, 16, 512], P('dir', 'batch')
- input_grad: float32 [256, 16, 512], P('batch')
- w_input_grad: float32 [2, 512, 4, 4096], P('dir', None, None, 'unit')
- w_hidden_grad: float32 [2, 512, 4, 4096], P('dir', None, None, 'unit')
- bias_grad: float32 [2, 4, 4096], P('dir', None, 'unit')
- w_proj_grad: float32 [2, 4096, 512], P('dir', 'unit')
- hidden_final: float32 [2, 256, 512], P('dir', 'batch')
- cell_final: float32 [2, 256, 4096], P('dir', 'batch', 'unit')
Inputs may be any that keep to these rules, and one draw needn't show every extreme that they name: `win_count`: stream 0 has 2 live windows and stream 1 has one. `last_live`: stream 0's last live window is full and stream 1's has one live step.
All inputs are finite; a program needn't handle non-finite values.
Results may differ from a plain program's by a relative error of at most 0.035.
Values may be sent and summed in bfloat16 or wider, within the bound.
A program may use at most 384 MiB of HBM per device.

v0:
```python
import jax
import jax.numpy as jnp
from jax import lax
from jax.sharding import PartitionSpec as P

WIN = 8
WINS = 2


def gate_cells(joined, w_both, bias_flat, cell_prev, cell_count):
    gates_pre = jnp.dot(joined, w_both, preferred_element_type=jnp.float32) + bias_flat
    gates_pre = gates_pre.reshape(joined.shape[0], 4, cell_count)
    in_gate = jax.nn.sigmoid(gates_pre[:, 0])
    forget_gate = jax.nn.sigmoid(gates_pre[:, 1])
    cand_gate = jnp.tanh(gates_pre[:, 2])
    out_gate = jax.nn.sigmoid(gates_pre[:, 3])
    cell_sum = forget_gate * cell_prev + in_gate * cand_gate
    cell_new = 3.0 * jnp.tanh(cell_sum / 3.0)
    cell_low = (out_gate * jnp.tanh(cell_new)).astype(jnp.bfloat16)
    return (in_gate, forget_gate, cand_gate, out_gate, cell_sum, cell_new, cell_low)


def on_device(
    inputs,
    win_count,
    last_live,
    hidden_init,
    cell_init,
    w_input,
    w_hidden,
    gate_bias,
    w_proj,
    out_grad,
):
    unit_count = lax.axis_size("unit")
    unit_index = lax.axis_index("unit")
    stream_count = inputs.shape[0]
    step_count = inputs.shape[1]
    model_width = inputs.shape[2]
    cell_count = w_input.shape[3]
    row_count = stream_count // unit_count
    row_start = unit_index * row_count
    flipped = lax.axis_index("dir") == 1
    seq_length = (win_count - 1) * WIN + last_live
    live_mask = (
        lax.broadcasted_iota(jnp.int32, (stream_count, step_count), 1) < seq_length[:, None]
    ).astype(jnp.float32)
    inputs_seq = jnp.where(flipped, inputs[:, ::-1], inputs)
    live_seq = jnp.where(flipped, live_mask[:, ::-1], live_mask)
    grad_seq = jnp.where(flipped, out_grad[0][:, ::-1], out_grad[0])
    inputs_time = jnp.swapaxes(inputs_seq, 0, 1)
    mask_time = jnp.swapaxes(live_seq, 0, 1)[:, :, None]
    grad_time = jnp.swapaxes(grad_seq, 0, 1).astype(jnp.float32)
    w_in_flat = w_input[0].reshape(model_width, 4 * cell_count)
    w_hid_flat = w_hidden[0].reshape(model_width, 4 * cell_count)
    w_both = jnp.concatenate([w_in_flat, w_hid_flat], 0)
    bias_flat = gate_bias[0].reshape(4 * cell_count)
    proj_local = w_proj[0]
    proj_full = lax.all_gather(proj_local, "unit", axis=0, tiled=True)

    def project(cell_low):
        cell_rows = lax.all_to_all(cell_low, "unit", split_axis=0, concat_axis=1, tiled=True)
        proj_pre = jnp.dot(cell_rows, proj_full, preferred_element_type=jnp.float32)
        hidden_mine = (3.0 * jnp.tanh(proj_pre / 3.0)).astype(jnp.bfloat16)
        hidden_all = lax.all_gather(hidden_mine, "unit", axis=0, tiled=True)
        return (hidden_all, cell_rows, proj_pre)

    def window_forward(start_state, input_block, mask_block, keep_all):

        def advance(state_in, step_data):
            hidden_low, cell_prev = state_in
            input_now, mask_now = step_data
            joined = jnp.concatenate([input_now, hidden_low], 1)
            in_gate, forget_gate, cand_gate, out_gate, cell_sum, cell_new, cell_low = gate_cells(
                joined, w_both, bias_flat, cell_prev, cell_count
            )
            hidden_all, cell_rows, proj_pre = project(cell_low)
            hidden_next = jnp.where(mask_now > 0, hidden_all, hidden_low)
            cell_next = jnp.where(mask_now > 0, cell_new, cell_prev)
            if keep_all:
                kept = (
                    joined,
                    cell_prev,
                    in_gate,
                    forget_gate,
                    cand_gate,
                    out_gate,
                    cell_sum,
                    cell_new,
                    cell_rows,
                    proj_pre,
                )
            else:
                kept = (
                    input_now.astype(jnp.float32) + mask_now * hidden_all.astype(jnp.float32)
                ).astype(jnp.bfloat16)
            return ((hidden_next, cell_next), kept)

        return lax.scan(advance, start_state, (input_block, mask_block))

    def retreat(state_in, step_data):
        grad_hidden, grad_cell, acc_cat, acc_bias, acc_proj = state_in
        (
            joined,
            cell_prev,
            in_gate,
            forget_gate,
            cand_gate,
            out_gate,
            cell_sum,
            cell_new,
            cell_rows,
            proj_pre,
            mask_now,
            grad_now,
        ) = step_data
        mask_mine = lax.dynamic_slice_in_dim(mask_now, row_start, row_count, 0)
        grad_mine = lax.dynamic_slice_in_dim(grad_now, row_start, row_count, 0)
        grad_out = mask_mine * (grad_mine + grad_hidden)
        squash = jnp.tanh(proj_pre / 3.0)
        grad_pre = (grad_out * (1.0 - squash * squash)).astype(jnp.bfloat16)
        acc_proj = acc_proj + lax.dot_general(
            cell_rows, grad_pre, (((0,), (0,)), ((), ())), preferred_element_type=jnp.float32
        )
        grad_rows = lax.dot_general(
            grad_pre, proj_full, (((1,), (1,)), ((), ())), preferred_element_type=jnp.float32
        ).astype(jnp.bfloat16)
        grad_cells_low = lax.all_to_all(grad_rows, "unit", split_axis=1, concat_axis=0, tiled=True)
        grad_mout = grad_cells_low.astype(jnp.float32)
        cell_tanh = jnp.tanh(cell_new)
        grad_new = mask_now * grad_cell + grad_mout * out_gate * (1.0 - cell_tanh * cell_tanh)
        sum_tanh = jnp.tanh(cell_sum / 3.0)
        grad_inner = grad_new * (1.0 - sum_tanh * sum_tanh)
        gate_grad = (
            jnp.stack(
                [
                    grad_inner * cand_gate * in_gate * (1.0 - in_gate),
                    grad_inner * cell_prev * forget_gate * (1.0 - forget_gate),
                    grad_inner * in_gate * (1.0 - cand_gate * cand_gate),
                    grad_mout * cell_tanh * out_gate * (1.0 - out_gate),
                ],
                1,
            )
            .reshape(stream_count, 4 * cell_count)
            .astype(jnp.bfloat16)
        )
        grad_cell_prev = (1.0 - mask_now) * grad_cell + grad_inner * forget_gate
        acc_cat = acc_cat + lax.dot_general(
            joined, gate_grad, (((0,), (0,)), ((), ())), preferred_element_type=jnp.float32
        )
        acc_bias = acc_bias + jnp.sum(gate_grad.astype(jnp.float32), 0)
        partial_hidden = lax.dot_general(
            gate_grad, w_hid_flat, (((1,), (1,)), ((), ())), preferred_element_type=jnp.float32
        )
        back_hidden = lax.psum_scatter(
            partial_hidden.astype(jnp.bfloat16), "unit", scatter_dimension=0, tiled=True
        ).astype(jnp.float32)
        grad_hidden_prev = (1.0 - mask_mine) * grad_hidden + back_hidden
        return ((grad_hidden_prev, grad_cell_prev, acc_cat, acc_bias, acc_proj), gate_grad)

    state = (hidden_init[0].astype(jnp.bfloat16), cell_init[0])
    edges = []
    outputs = []
    for window in range(WINS):
        edges.append(state)
        state, out_block = window_forward(
            state,
            inputs_time[window * WIN : (window + 1) * WIN],
            mask_time[window * WIN : (window + 1) * WIN],
            False,
        )
        outputs.append(out_block)
    hidden_last, cell_last = state
    output_seq = jnp.swapaxes(jnp.concatenate(outputs, 0), 0, 1)
    layer_out = jnp.where(flipped, output_seq[:, ::-1], output_seq)[None]
    grad_hidden = jnp.zeros((row_count, model_width), jnp.float32)
    grad_cell = jnp.zeros((stream_count, cell_count), jnp.float32)
    total_cat = jnp.zeros((2 * model_width, 4 * cell_count), jnp.float32)
    total_bias = jnp.zeros((4 * cell_count,), jnp.float32)
    total_proj = jnp.zeros(proj_full.shape, jnp.float32)
    input_parts = [None] * WINS
    for window in reversed(range(WINS)):
        lower = window * WIN
        upper = (window + 1) * WIN
        unused_state, kept = window_forward(
            edges[window], inputs_time[lower:upper], mask_time[lower:upper], True
        )
        start_grads = (
            grad_hidden,
            grad_cell,
            jnp.zeros_like(total_cat),
            jnp.zeros_like(total_bias),
            jnp.zeros_like(total_proj),
        )
        finished, gate_grads = lax.scan(
            retreat,
            start_grads,
            kept + (mask_time[lower:upper], grad_time[lower:upper]),
            reverse=True,
        )
        grad_hidden, grad_cell, window_cat, window_bias, window_proj = finished
        input_parts[window] = lax.dot_general(
            gate_grads, w_in_flat, (((2,), (1,)), ((), ())), preferred_element_type=jnp.float32
        )
        total_cat = total_cat + window_cat
        total_bias = total_bias + window_bias
        total_proj = total_proj + window_proj
    input_time = jnp.concatenate(input_parts, 0) + jnp.where(unit_index == 0, grad_time, 0.0)
    input_seq = jnp.swapaxes(input_time, 0, 1)
    input_seq = jnp.where(flipped, input_seq[:, ::-1], input_seq)
    input_grad = lax.psum(input_seq.astype(jnp.bfloat16), ("dir", "unit")).astype(jnp.float32)
    total_proj = lax.psum_scatter(
        total_proj.astype(jnp.bfloat16), "unit", scatter_dimension=0, tiled=True
    ).astype(jnp.float32)
    total_cat, total_bias, total_proj = (
        lax.psum(total_cat.astype(jnp.bfloat16), "batch").astype(jnp.float32),
        lax.psum(total_bias.astype(jnp.bfloat16), "batch").astype(jnp.float32),
        lax.psum(total_proj.astype(jnp.bfloat16), "batch").astype(jnp.float32),
    )
    w_input_grad = total_cat[:model_width].reshape(model_width, 4, cell_count)[None]
    w_hidden_grad = total_cat[model_width:].reshape(model_width, 4, cell_count)[None]
    bias_grad = total_bias.reshape(4, cell_count)[None]
    return (
        layer_out,
        input_grad,
        w_input_grad,
        w_hidden_grad,
        bias_grad,
        total_proj[None],
        hidden_last.astype(jnp.float32)[None],
        cell_last[None],
    )


def solution(mesh):
    placed = (
        P("batch", None, None),
        P("batch"),
        P("batch"),
        P("dir", "batch", None),
        P("dir", "batch", "unit"),
        P("dir", None, None, "unit"),
        P("dir", None, None, "unit"),
        P("dir", None, "unit"),
        P("dir", "unit", None),
        P("dir", "batch", None, None),
    )
    return jax.shard_map(
        on_device,
        mesh=mesh,
        in_specs=placed,
        out_specs=(
            P("dir", "batch", None, None),
            P("batch", None, None),
            P("dir", None, None, "unit"),
            P("dir", None, None, "unit"),
            P("dir", None, "unit"),
            P("dir", "unit", None),
            P("dir", "batch", None),
            P("dir", "batch", "unit"),
        ),
        check_vma=False,
    )
```

profile of v0, /device:TPU:0, one launch (start us, length us, event | category | flops | bytes accessed | tf_op | source)
XLA Modules:
  0.0 2619.5 jit_solution(3949649254816250251)
XLA Ops:
  69.8 228.0 %while.144 = (s32[]{:T(128)}, bf16[32,512]{1,0:T(8,128)(2,1)S(1)}, f32[32,2048]{1,0:T(8,128)S(1)}, bf16[8,32,512]{2,1,0:T(8,128)(2,1)}, f32[8,32,1]{1,2,0:T(1,12...) while((s32[]{:T(128)}, bf16[32,512]{1,0:T(8,128)(2,1)S(1)}, ...), condition=%wide.region_1.2_spmd, body=%wide.region_0.1_spmd.sunk | while | flops 605610048 | bytes 29721208 | solution.py:99
  311.3 312.7 %while.146 = (s32[]{:T(128)}, bf16[32,512]{1,0:T(8,128)(2,1)S(1)}, f32[32,2048]{1,0:T(8,128)S(1)}, bf16[8,32,1024]{2,1,0:T(8,128)(2,1)}, f32[8,32,2048]{2,1,0:T(...) while((s32[]{:T(128)}, bf16[32,512]{1,0:T(8,128)(2,1)S(1)}, ...), condition=%wide.region_5.6_spmd, body=%wide.region_4.5_spmd.sunk | while | flops 606380032 | bytes 36405732 | solution.py:99
  626.5 450.0 %while.148 = (s32[]{:T(128)}, f32[16,512]{1,0:T(8,128)S(1)}, f32[32,2048]{1,0:T(8,128)S(1)}, f32[1024,8192]{1,0:T(8,128)}, f32[8192]{0:T(1024)S(1)}, /*index=5*/...) while((s32[]{:T(128)}, f32[16,512]{1,0:T(8,128)S(1)}, ...), condition=%wide.region_9.10_spmd.clone, body=%wide.region_6.9_spmd.clone.sunk | while | flops 964419648 | bytes 114104064 | solution.py:195
  702.4 24.7 select_add_fusion.12
  760.3 24.7 select_add_fusion.12
  818.3 24.7 select_add_fusion.12
  876.3 24.7 select_add_fusion.12
  934.3 24.7 select_add_fusion.12
  992.2 24.7 select_add_fusion.12
  1050.2 24.7 select_add_fusion.12
  1089.4 323.8 %while.147 = (s32[]{:T(128)}, bf16[32,512]{1,0:T(8,128)(2,1)S(1)}, f32[32,2048]{1,0:T(8,128)S(1)}, bf16[8,32,1024]{2,1,0:T(8,128)(2,1)S(1)}, f32[8,32,2048]{2,1,...) while((s32[]{:T(128)}, bf16[32,512]{1,0:T(8,128)(2,1)S(1)}, ...), condition=%wide.region_11.12_spmd, body=%wide.region_10.11_spmd.sunk | while | flops 606380032 | bytes 36405732 | solution.py:99
  1415.6 460.4 %while.149 = (s32[]{:T(128)}, f32[16,512]{1,0:T(8,128)S(1)}, f32[32,2048]{1,0:T(8,128)S(1)}, f32[1024,8192]{1,0:T(8,128)}, f32[8192]{0:T(1024)S(1)}, /*index=5*/...) while((s32[]{:T(128)}, f32[16,512]{1,0:T(8,128)S(1)}, ...), condition=%wide.region_15.16_spmd.clone, body=%wide.region_12.15_spmd.clone.sunk | while | flops 964329536 | bytes 114102640 | solution.py:195
  1493.4 24.7 select_add_fusion.15
  1552.8 24.7 select_add_fusion.15
  1612.2 24.7 select_add_fusion.15
  1671.5 24.7 select_add_fusion.15
  1730.9 24.7 select_add_fusion.15
  1790.4 24.7 select_add_fusion.15
  1849.7 24.7 select_add_fusion.15
  1912.4 28.1 %add_convert_fusion.2 = bf16[1024,8192]{1,0:T(8,128)(2,1)} fusion(f32[1024,8192]{1,0:T(8,128)} %get-tuple-element.1342, f32[1024,8192]{1,0:T(8,128)} %get-tuple-element.1343), kind=kLoop, calls=%fused_computation.260 | loop fusion | flops 16777216 | bytes 83886080 | tf_op jit(solution)/shard_map/convert_element_type | solution.py:216
  1942.1 233.1 %while.145 = (s32[]{:T(128)}, bf16[32,512]{1,0:T(8,128)(2,1)S(1)}, f32[32,2048]{1,0:T(8,128)S(1)}, bf16[8,32,512]{2,1,0:T(8,128)(2,1)S(1)}, f32[8,32,1]{1,2,0:T(...) while((s32[]{:T(128)}, bf16[32,512]{1,0:T(8,128)(2,1)S(1)}, ...), condition=%wide.region_3.4_spmd, body=%wide.region_2.3_spmd.sunk | while | flops 605610048 | bytes 29721592 | solution.py:99
  2176.6 38.7 %psum.30 = bf16[1,4,2048]{2,1,0:T(4,128)(2,1)S(1)} all-reduce(bf16[1,4,2048]{2,1,0:T(4,128)(2,1)S(1)} %broadcast_in_dim_reshape.14), channel_id=1, replica_groups=mesh['dir'=2,'batch'=8,'unit'=2] {'batch'}, use_global_device_ids=true, to_apply=%region_18.19 | all-reduce | flops 8192 | bytes 32768 | tf_op jit(solution)/shard_map/psum | solution.py:217
  2218.8 333.0 %all-reduce.6.cloned.1.call-done = (bf16[1024,8192]{1,0:T(8,128)(2,1)}, bf16[1,2048,512]{2,1,0:T(8,128)(2,1)}) async-done(((bf16[1024,8192]{1,0:T(8,128)(2,1)}, bf16[1,2048,512]{2,1,0:T(8,128)(2,1)}), (bf16[1024,8192]{1,0:T(8,128)(2,1)}, bf16[1,2048,512]{2,1,0:T(8,128)(2,1)})) %all-reduce.6.cloned.1.call-update) | async-done | bytes 18874384 | tf_op jit(solution)/shard_map/psum | solution.py:216
  2589.1 20.6 broadcast_in_dim_reshape.13
  (1204 shorter events, 1825.0 us)
Async XLA Ops:
  7.2 61.9 %all-gather.3.cloned.1.call-start = ((), (), s32[]{:S(2)}) async-start(), calls=%async_computation.11 | async-start | bytes 6291456 | tf_op jit(solution)/shard_map/all_gather | solution.py:59
  362.8 18.6 all-to-all-start.2
  440.9 18.6 all-to-all-start.2
  479.9 18.6 all-to-all-start.2
  597.2 18.6 all-to-all-start.2
  634.3 35.7 %reduce-scatter.6.cloned.1.call-start = ((), (), s32[]{:S(2)}) async-start(), calls=%async_computation.13 | async-start | bytes 49152 | tf_op jit(solution)/shard_map/while/body/eval_jaxpr/reduce_scatter | solution.py:155
  678.3 49.6 %reduce-scatter.6.cloned.1.call-start = ((), (), s32[]{:S(2)}) async-start(), calls=%async_computation.13 | async-start | bytes 49152 | tf_op jit(solution)/shard_map/while/body/eval_jaxpr/reduce_scatter | solution.py:155
  736.3 49.6 %reduce-scatter.6.cloned.1.call-start = ((), (), s32[]{:S(2)}) async-start(), calls=%async_computation.13 | async-start | bytes 49152 | tf_op jit(solution)/shard_map/while/body/eval_jaxpr/reduce_scatter | solution.py:155
  794.2 49.6 %reduce-scatter.6.cloned.1.call-start = ((), (), s32[]{:S(2)}) async-start(), calls=%async_computation.13 | async-start | bytes 49152 | tf_op jit(solution)/shard_map/while/body/eval_jaxpr/reduce_scatter | solution.py:155
  852.2 49.6 %reduce-scatter.6.cloned.1.call-start = ((), (), s32[]{:S(2)}) async-start(), calls=%async_computation.13 | async-start | bytes 49152 | tf_op jit(solution)/shard_map/while/body/eval_jaxpr/reduce_scatter | solution.py:155
  910.2 49.6 %reduce-scatter.6.cloned.1.call-start = ((), (), s32[]{:S(2)}) async-start(), calls=%async_computation.13 | async-start | bytes 49152 | tf_op jit(solution)/shard_map/while/body/eval_jaxpr/reduce_scatter | solution.py:155
  968.1 49.6 %reduce-scatter.6.cloned.1.call-start = ((), (), s32[]{:S(2)}) async-start(), calls=%async_computation.13 | async-start | bytes 49152 | tf_op jit(solution)/shard_map/while/body/eval_jaxpr/reduce_scatter | solution.py:155
  1026.1 49.6 %reduce-scatter.6.cloned.1.call-start = ((), (), s32[]{:S(2)}) async-start(), calls=%async_computation.13 | async-start | bytes 49152 | tf_op jit(solution)/shard_map/while/body/eval_jaxpr/reduce_scatter | solution.py:155
  1424.0 35.6 %reduce-scatter.8.cloned.1.call-start = ((), (), s32[]{:S(2)}) async-start(), calls=%async_computation.14 | async-start | bytes 49152 | tf_op jit(solution)/shard_map/while/body/eval_jaxpr/reduce_scatter | solution.py:155
  1468.6 50.4 %reduce-scatter.8.cloned.1.call-start = ((), (), s32[]{:S(2)}) async-start(), calls=%async_computation.14 | async-start | bytes 49152 | tf_op jit(solution)/shard_map/while/body/eval_jaxpr/reduce_scatter | solution.py:155
  1528.0 50.4 %reduce-scatter.8.cloned.1.call-start = ((), (), s32[]{:S(2)}) async-start(), calls=%async_computation.14 | async-start | bytes 49152 | tf_op jit(solution)/shard_map/while/body/eval_jaxpr/reduce_scatter | solution.py:155
  1587.4 50.4 %reduce-scatter.8.cloned.1.call-start = ((), (), s32[]{:S(2)}) async-start(), calls=%async_computation.14 | async-start | bytes 49152 | tf_op jit(solution)/shard_map/while/body/eval_jaxpr/reduce_scatter | solution.py:155
  1646.7 50.3 %reduce-scatter.8.cloned.1.call-start = ((), (), s32[]{:S(2)}) async-start(), calls=%async_computation.14 | async-start | bytes 49152 | tf_op jit(solution)/shard_map/while/body/eval_jaxpr/reduce_scatter | solution.py:155
  1706.1 50.4 %reduce-scatter.8.cloned.1.call-start = ((), (), s32[]{:S(2)}) async-start(), calls=%async_computation.14 | async-start | bytes 49152 | tf_op jit(solution)/shard_map/while/body/eval_jaxpr/reduce_scatter | solution.py:155
  1765.5 50.4 %reduce-scatter.8.cloned.1.call-start = ((), (), s32[]{:S(2)}) async-start(), calls=%async_computation.14 | async-start | bytes 49152 | tf_op jit(solution)/shard_map/while/body/eval_jaxpr/reduce_scatter | solution.py:155
  1824.9 50.3 %reduce-scatter.8.cloned.1.call-start = ((), (), s32[]{:S(2)}) async-start(), calls=%async_computation.14 | async-start | bytes 49152 | tf_op jit(solution)/shard_map/while/body/eval_jaxpr/reduce_scatter | solution.py:155
  1876.0 65.1 %reduce-scatter.4.cloned.1.call-start = ((), (), s32[]{:S(2)}) async-start(), calls=%async_computation.10 | async-start | bytes 6291456 | tf_op jit(solution)/shard_map/reduce_scatter | solution.py:212
  1885.3 331.1 %all-reduce.4.cloned.1.call-start = ((), (), s32[]{:S(2)}) async-start(), calls=%async_computation.9 | async-start | bytes 1048576 | tf_op jit(solution)/shard_map/psum | solution.py:211
  1912.3 639.5 %all-reduce.6.cloned.1.call-start = ((), (), s32[]{:S(2)}) async-start(), calls=%async_computation.12 | async-start | bytes 37748736 | tf_op jit(solution)/shard_map/psum | solution.py:216
  (69 other events, 1622.6 us)
Sparse Core Ops, SparseCore 0:
  9.6 59.4 all-gather.2
  655.5 11.2 reduce-scatter.5
  702.1 11.1 reduce-scatter.5
  760.1 11.1 reduce-scatter.5
  818.0 11.1 reduce-scatter.5
  876.0 11.1 reduce-scatter.5
  934.0 11.1 reduce-scatter.5
  991.9 11.1 reduce-scatter.5
  1049.9 11.1 reduce-scatter.5
  1446.0 11.2 reduce-scatter.7
  1493.2 11.1 reduce-scatter.7
  1552.5 11.1 reduce-scatter.7
  1612.0 11.1 reduce-scatter.7
  1671.2 11.1 reduce-scatter.7
  1730.6 11.1 reduce-scatter.7
  1790.1 11.1 reduce-scatter.7
  1849.4 11.1 reduce-scatter.7
  1885.5 55.6 reduce-scatter.3
  1944.2 33.2 all-reduce.3
  1982.7 569.0 all-reduce.5
where the time goes:
time: 2650 us; the launch traced here: 2620 us
  matrix products  1040 us (39%)
  local copies, waits for them, and re-layouts  567 us (21%)
  waiting for transfers between devices  412 us (16%)
  other arithmetic  229 us (9%)
  blocking collectives  180 us (7%)
  starting transfers between devices  163 us (6%)
    dot_general x16, matrix products, retreat(): lax.dot_general(joined, gate_grad, (((0,), (0,)), ((), ())), preferred_el...  371 us
    psum x1, waiting for transfers between devices, on_device(): lax.psum(total_cat.astype(jnp.bfloat16), 'batch').astype(jnp.float32)  333 us
    dot_general x32, matrix products, gate_cells(): jnp.dot(joined, w_both, preferred_element_type=jnp.float32) + bias_flat  282 us
    dynamic_update_slice x96, local copies, waits for them, and re-layouts, window_forward(): return lax.scan(advance, start_state, (input_block, mask_block))  223 us
    all_gather x32, blocking collectives, project(): hidden_all = lax.all_gather(hidden_mine, 'unit', axis=0, tiled=True)  142 us
    dot_general x16, matrix products, retreat(): lax.dot_general(cell_rows, grad_pre, (((0,), (0,)), ((), ())), preferred_...  125 us
    all_to_all x32, starting transfers between devices, project(): lax.all_to_all(cell_low, 'unit', split_axis=0, concat_axis=1, tiled=True)  108 us
    dot_general x16, matrix products, retreat(): lax.dot_general(gate_grad, w_hid_flat, (((1,), (1,)), ((), ())), preferre...  106 us
  transfers between devices with their start and end apart: 68, of which 19 were waited for; matrix products, arithmetic and copies ran while one was open for 41% of the time, Pallas kernels for 0%

commit v1 on v0

v1 whole, which is shorter than its diff:
```python
import functools

import jax
import jax.numpy as jnp
from jax import lax
from jax.experimental import pallas as pl
from jax.experimental.pallas import tpu as pltpu
from jax.sharding import PartitionSpec as P

WIN = 8
BLK = 256
RING = 4
MESH = pl.DeviceIdType.MESH
BF = jnp.bfloat16
F32 = jnp.float32
NT = (((1,), (1,)), ((), ()))
VMEM_LIMIT = 60 * 1024 * 1024
THIRD = 1.0 / 3.0


def sigmoid(v):
    return 0.5 * jnp.tanh(0.5 * v) + 0.5


def mm(a, b):
    return jnp.dot(a, b, preferred_element_type=F32)


def mm_nt(a, b):
    return lax.dot_general(a, b, NT, preferred_element_type=F32)


def identity():
    rows = lax.broadcasted_iota(jnp.int32, (BLK, BLK), 0)
    cols = lax.broadcasted_iota(jnp.int32, (BLK, BLK), 1)
    return jnp.where(rows == cols, 1.0, 0.0).astype(BF)


def gate_order():
    rows = lax.broadcasted_iota(jnp.int32, (BLK, BLK), 0)
    cols = lax.broadcasted_iota(jnp.int32, (BLK, BLK), 1)
    want = (rows & (BLK // 4 - 1)) * 4 + (rows >> 6)
    return jnp.where(want == cols, 1.0, 0.0).astype(BF)


def recurrence_kernel(
    x_ref,
    y_ref,
    len_ref,
    h0_ref,
    c0_ref,
    bias_ref,
    wx_hbm,
    wh_hbm,
    wp_hbm,
    lay_ref,
    hfin_ref,
    cfin_ref,
    dx_ref,
    dzg,
    xhg,
    mg,
    drg,
    wx,
    wh,
    wht,
    wp,
    wpt,
    raw,
    z,
    c,
    th,
    h,
    m,
    dr,
    dz,
    dc,
    dh,
    snd,
    rcv,
    load_sem,
    ex_send,
    ex_recv,
    y_send,
    y_recv,
    own_sem,
    x_sem,
):
    steps, streams, width = x_ref.shape
    units = wp.shape[0]
    tiles = units // BLK
    gate4 = 4 * BLK
    half_cols = 2 * units
    half_units = units // 2
    flip = lax.axis_index("dir")
    batch = lax.axis_index("batch")
    unit = lax.axis_index("unit")
    mine = lax.rem(batch, 2)
    other = 1 - mine
    y_dev = {"batch": batch + 1 - 2 * mine}
    x_dev = {"unit": 1 - unit}

    def place(t):
        return t + flip * (steps - 1 - 2 * t)

    barrier = pltpu.get_barrier_semaphore()
    pl.semaphore_signal(barrier, 1, device_id=x_dev, device_id_type=MESH)
    pl.semaphore_signal(barrier, 1, device_id=y_dev, device_id_type=MESH)

    blocks = width * 4 // BLK
    proj_copy = pltpu.make_async_copy(wp_hbm, wp, load_sem.at[2])
    proj_copy.start()

    def load(w_hbm, b, slot):
        return pltpu.make_async_copy(
            w_hbm.reshape(width * 4, units).at[pl.ds(pl.multiple_of(b * BLK, BLK), BLK)],
            raw.at[slot],
            load_sem.at[slot],
        )

    order = gate_order()

    def spread(w_hbm, w):
        def body(b, carry):
            slot = lax.rem(b, 2)

            @pl.when(b + 1 < blocks)
            def _():
                load(w_hbm, b + 1, 1 - slot).start()

            load(w_hbm, b, slot).wait()
            for j in range(tiles):
                got = mm(order, raw[slot, :, j * BLK : (j + 1) * BLK]).astype(BF)
                for g in range(4):
                    col = j * gate4 + g * BLK
                    w[pl.ds(pl.multiple_of(b * 64, 64), 64), col : col + BLK] = got[
                        g * 64 : (g + 1) * 64
                    ]
            return carry

        load(w_hbm, 0, 0).start()
        lax.fori_loop(0, blocks, body, 0)

    spread(wx_hbm, wx)
    spread(wh_hbm, wh)

    pl.semaphore_wait(barrier, 2)
    x_remote = pltpu.make_async_remote_copy(
        x_ref,
        xhg.at[mine, :, :, pl.ds(0, width)],
        x_sem.at[0],
        x_sem.at[1],
        device_id=y_dev,
        device_id_type=MESH,
    )
    x_local = pltpu.make_async_copy(x_ref, xhg.at[mine, :, :, pl.ds(0, width)], x_sem.at[2])
    x_remote.start()
    x_local.start()

    def exchange(k):
        slot = lax.rem(k, 2)
        return pltpu.make_async_remote_copy(
            snd.at[slot],
            rcv.at[slot],
            ex_send.at[slot],
            ex_recv.at[slot],
            device_id=x_dev,
            device_id_type=MESH,
        )

    def pair(kind, t, away, keep, target):
        return (
            pltpu.make_async_remote_copy(
                away,
                target,
                y_send.at[kind, t],
                y_recv.at[kind, t],
                device_id=y_dev,
                device_id_type=MESH,
            ),
            pltpu.make_async_copy(keep, target, own_sem.at[kind, t]),
        )

    def h_pair(t):
        return pair(0, t, h.at[t], h.at[t], xhg.at[mine, place(t), :, pl.ds(width, width)])

    def m_pair(t):
        slot = lax.rem(t, RING)
        away = m.at[slot, :, pl.ds(pl.multiple_of(other * half_units, half_units), half_units)]
        keep = m.at[slot, :, pl.ds(pl.multiple_of(mine * half_units, half_units), half_units)]
        return pair(1, t, away, keep, mg.at[mine, place(t)])

    def dr_pair(t):
        return pair(2, t, dr.at[t], dr.at[t], drg.at[mine, place(t)])

    def dz_pair(t):
        slot = lax.rem(t, RING)
        away = dz.at[slot, :, pl.ds(pl.multiple_of(other * half_cols, half_cols), half_cols)]
        keep = dz.at[slot, :, pl.ds(pl.multiple_of(mine * half_cols, half_cols), half_cols)]
        return pair(3, t, away, keep, dzg.at[mine, place(t)])

    def begin(copies):
        for one in copies:
            one.start()

    def sent(copies):
        copies[0].wait_send()
        copies[1].wait()

    def live_of(t, cols):
        live = jnp.where(len_ref[...] > place(t), 1.0, 0.0)
        return jnp.concatenate([live] * (cols // 128), 1)

    def input_part(t):
        now = x_ref[place(t)]
        for j in range(tiles):
            part = mm(now, wx[:, j * gate4 : (j + 1) * gate4])
            for g in range(4):
                z[t, :, j * gate4 + g * BLK : j * gate4 + (g + 1) * BLK] = (
                    part[:, g * BLK : (g + 1) * BLK] + bias_ref[g : g + 1, j * BLK : (j + 1) * BLK]
                )

    eye = identity()
    h[0] = h0_ref[...].astype(BF)
    c[0] = c0_ref[...]
    input_part(0)
    proj_copy.wait()
    turn_cols = 4 * units // steps
    turn_units = units // steps

    def forward(t, carry):
        slot = lax.rem(t, RING)

        @pl.when(t >= RING)
        def _():
            sent(m_pair(t - RING))

        live = live_of(t, BLK) > 0.5
        hidden = h[t]
        for j in range(tiles):
            cols = slice(j * BLK, (j + 1) * BLK)
            base = j * gate4
            pre = z[t, :, base : base + gate4] + mm(hidden, wh[:, base : base + gate4])
            in_gate = sigmoid(pre[:, :BLK])
            forget = sigmoid(pre[:, BLK : 2 * BLK])
            cand = jnp.tanh(pre[:, 2 * BLK : 3 * BLK])
            out_gate = sigmoid(pre[:, 3 * BLK :])
            prev = c[t, :, cols]
            new = 3.0 * jnp.tanh((forget * prev + in_gate * cand) * THIRD)
            m[slot, :, cols] = (out_gate * jnp.tanh(new)).astype(BF)
            z[t, :, base : base + BLK] = in_gate
            z[t, :, base + BLK : base + 2 * BLK] = forget
            z[t, :, base + 2 * BLK : base + 3 * BLK] = cand
            z[t, :, base + 3 * BLK : base + gate4] = out_gate
            c[t + 1, :, cols] = jnp.where(live, new, prev)
        two = lax.rem(t, 2)
        snd[two] = mm(m[slot], wp[...]).astype(BF)
        copy = exchange(t)
        copy.start()
        begin(h_pair(t))
        begin(m_pair(t))

        @pl.when(t + 1 < steps)
        def _():
            input_part(t + 1)

        at = pl.multiple_of(t * turn_cols, turn_cols)
        for kb in range(width // BLK):
            for cb in range(turn_cols // BLK):
                wht[pl.ds(at + cb * BLK, BLK), kb * BLK : (kb + 1) * BLK] = mm_nt(
                    eye, wh[kb * BLK : (kb + 1) * BLK, pl.ds(at + cb * BLK, BLK)]
                ).astype(BF)
        at = pl.multiple_of(t * turn_units, turn_units)
        for kb in range(width // BLK):
            wpt[kb * BLK : (kb + 1) * BLK, pl.ds(at, turn_units)] = mm_nt(
                eye, wp[pl.ds(at, turn_units), kb * BLK : (kb + 1) * BLK]
            ).astype(BF)
        copy.wait()
        total = snd[two].astype(F32) + rcv[two].astype(F32)
        squash = jnp.tanh(total * THIRD)
        th[t] = squash
        new_hidden = (3.0 * squash).astype(BF)
        live_h = live_of(t, width)
        lay_ref[place(t)] = (
            x_ref[place(t)].astype(F32) + live_h * new_hidden.astype(F32)
        ).astype(BF)
        h[t + 1] = jnp.where(live_h > 0.5, new_hidden.astype(F32), hidden.astype(F32)).astype(BF)
        return carry

    lax.fori_loop(0, steps, forward, 0)
    hfin_ref[...] = h[steps].astype(F32)
    cfin_ref[...] = c[steps]

    dc[...] = jnp.zeros_like(dc)
    dh[...] = jnp.zeros_like(dh)

    def backward(k, carry):
        t = steps - 1 - k
        slot = lax.rem(t, RING)

        @pl.when(k >= RING)
        def _():
            sent(dz_pair(t + RING))

        grad_hidden = dh[...]
        live_h = live_of(t, width)
        squash = th[t]
        y_now = y_ref[place(t)].astype(F32)
        low = (live_h * (y_now + grad_hidden) * (1.0 - squash * squash)).astype(BF)
        dr[t] = low
        live = live_of(t, BLK)
        part = jnp.zeros((streams, width), F32)
        for j in range(tiles):
            cols = slice(j * BLK, (j + 1) * BLK)
            base = j * gate4
            grad_m = mm(low, wpt[:, cols]).astype(BF).astype(F32)
            in_gate = z[t, :, base : base + BLK]
            forget = z[t, :, base + BLK : base + 2 * BLK]
            cand = z[t, :, base + 2 * BLK : base + 3 * BLK]
            out_gate = z[t, :, base + 3 * BLK : base + gate4]
            prev = c[t, :, cols]
            new = c[t + 1, :, cols]
            grad_c = dc[:, cols]
            tanh_new = jnp.tanh(new)
            grad_n = live * grad_c + grad_m * out_gate * (1.0 - tanh_new * tanh_new)
            third = new * THIRD
            grad_u = grad_n * (1.0 - third * third)
            dz[slot, :, base : base + BLK] = (grad_u * cand * in_gate * (1.0 - in_gate)).astype(BF)
            dz[slot, :, base + BLK : base + 2 * BLK] = (
                grad_u * prev * forget * (1.0 - forget)
            ).astype(BF)
            dz[slot, :, base + 2 * BLK : base + 3 * BLK] = (
                grad_u * in_gate * (1.0 - cand * cand)
            ).astype(BF)
            dz[slot, :, base + 3 * BLK : base + gate4] = (
                grad_m * tanh_new * out_gate * (1.0 - out_gate)
            ).astype(BF)
            dc[:, cols] = (1.0 - live) * grad_c + grad_u * forget
            part = part + mm(dz[slot, :, base : base + gate4], wht[base : base + gate4, :])
        two = lax.rem(k, 2)
        snd[two] = part.astype(BF)
        copy = exchange(k)
        copy.start()
        begin(dz_pair(t))
        begin(dr_pair(t))
        grad_x = y_now * jnp.where(unit == 0, 1.0, 0.0)
        for j in range(tiles):
            base = j * gate4
            grad_x = grad_x + mm_nt(dz[slot, :, base : base + gate4], wx[:, base : base + gate4])
        dx_ref[place(t)] = grad_x.astype(BF)
        copy.wait()
        dh[...] = (1.0 - live_h) * grad_hidden + (snd[two].astype(F32) + rcv[two].astype(F32))
        return carry

    lax.fori_loop(0, steps, backward, 0)

    def last_m(i, carry):
        sent(m_pair(steps - RING + i))
        sent(dz_pair(i))
        return carry

    lax.fori_loop(0, RING, last_m, 0)

    def finish(t, carry):
        sent(h_pair(t))
        sent(dr_pair(t))
        h_pair(t)[0].wait_recv()
        m_pair(t)[0].wait_recv()
        dr_pair(t)[0].wait_recv()
        dz_pair(t)[0].wait_recv()
        return carry

    lax.fori_loop(0, steps, finish, 0)
    x_remote.wait()
    x_local.wait()


def recurrence(x_time, y_time, lens, hidden0, cell0, bias, w_in, w_hid, proj):
    steps, streams, width = x_time.shape
    units = proj.shape[0]
    vmem = pl.BlockSpec(memory_space=pltpu.VMEM)
    hbm = pl.BlockSpec(memory_space=pl.ANY)
    shape = jax.ShapeDtypeStruct
    return pl.pallas_call(
        recurrence_kernel,
        out_shape=(
            shape((steps, streams, width), BF),
            shape((streams, width), F32),
            shape((streams, units), F32),
            shape((steps, streams, width), BF),
            shape((2, steps, streams, 2 * units), BF),
            shape((2, steps, streams, 2 * width), BF),
            shape((2, steps, streams, units // 2), BF),
            shape((2, steps, streams, width), BF),
        ),
        in_specs=[vmem] * 6 + [hbm] * 3,
        out_specs=(vmem, vmem, vmem, vmem, hbm, hbm, hbm, hbm),
        scratch_shapes=[
            pltpu.VMEM((width, 4 * units), BF),
            pltpu.VMEM((width, 4 * units), BF),
            pltpu.VMEM((4 * units, width), BF),
            pltpu.VMEM((units, width), BF),
            pltpu.VMEM((width, units), BF),
            pltpu.VMEM((2, BLK, units), BF),
            pltpu.VMEM((steps, streams, 4 * units), F32),
            pltpu.VMEM((steps + 1, streams, units), F32),
            pltpu.VMEM((steps, streams, width), F32),
            pltpu.VMEM((steps + 1, streams, width), BF),
            pltpu.VMEM((RING, streams, units), BF),
            pltpu.VMEM((steps, streams, width), BF),
            pltpu.VMEM((RING, streams, 4 * units), BF),
            pltpu.VMEM((streams, units), F32),
            pltpu.VMEM((streams, width), F32),
            pltpu.VMEM((2, streams, width), BF),
            pltpu.VMEM((2, streams, width), BF),
            pltpu.SemaphoreType.DMA((3,)),
            pltpu.SemaphoreType.DMA((2,)),
            pltpu.SemaphoreType.DMA((2,)),
            pltpu.SemaphoreType.DMA((4, steps)),
            pltpu.SemaphoreType.DMA((4, steps)),
            pltpu.SemaphoreType.DMA((4, steps)),
            pltpu.SemaphoreType.DMA((3,)),
        ],
        compiler_params=pltpu.CompilerParams(
            collective_id=0, has_side_effects=True, vmem_limit_bytes=VMEM_LIMIT
        ),
        name="recurrence",
    )(x_time, y_time, lens, hidden0, cell0, bias, w_in, w_hid, proj)


def gradient_kernel(
    lanes,
    dz_hbm,
    xh_hbm,
    m_hbm,
    dr_hbm,
    dx_ref,
    res,
    bres,
    ig_ref,
    dz,
    xh,
    xht,
    m,
    mt,
    dr,
    acc,
    own,
    from_left,
    from_right,
    bown,
    bleft,
    bright,
    rx,
    red,
    load_sem,
    l_recv,
    r_recv,
    y_recv,
    l_send,
    r_send,
    y_send,
    o_sem,
    g_send,
    g_recv,
):
    rows, cols = dz.shape
    depth = xh.shape[1]
    row_blocks = depth // BLK
    col_blocks = cols // BLK
    n_cat = row_blocks * col_blocks
    proj_cols = dr.shape[1] // BLK
    n_all = n_cat + (m.shape[1] // BLK) * proj_cols
    flip = lax.axis_index("dir")
    batch = lax.axis_index("batch")
    unit = lax.axis_index("unit")
    mine = lax.rem(batch, 2)
    lane = lax.div(batch, 2)
    mid = lanes // 2
    y_dev = {"batch": batch + 1 - 2 * mine}
    l_dev = {"batch": batch - 2}
    r_dev = {"batch": batch + 2}
    has_left = lane > 0
    has_right = lane < lanes - 1
    before = lane < mid
    after = lane > mid
    middle = lane == mid

    def group(o):
        return {
            "dir": flip + (o % 2) * (1 - 2 * flip),
            "unit": unit + (o // 2) * (1 - 2 * unit),
        }

    loads = [
        pltpu.make_async_copy(xh_hbm, xh, load_sem.at[0]),
        pltpu.make_async_copy(dz_hbm, dz, load_sem.at[1]),
        pltpu.make_async_copy(m_hbm, m, load_sem.at[2]),
        pltpu.make_async_copy(dr_hbm, dr, load_sem.at[3]),
    ]
    for one in loads:
        one.start()
    barrier = pltpu.get_barrier_semaphore()
    pl.semaphore_signal(barrier, 1, device_id=y_dev, device_id_type=MESH)
    for o in (1, 2, 3):
        pl.semaphore_signal(barrier, 1, device_id=group(o), device_id_type=MESH)

    @pl.when(has_left)
    def _():
        pl.semaphore_signal(barrier, 1, device_id=l_dev, device_id_type=MESH)

    @pl.when(has_right)
    def _():
        pl.semaphore_signal(barrier, 1, device_id=r_dev, device_id_type=MESH)

    eye = identity()

    def turn(src, dst):
        for a in range(src.shape[1] // BLK):
            for b in range(src.shape[0] // BLK):
                dst[a * BLK : (a + 1) * BLK, b * BLK : (b + 1) * BLK] = mm_nt(
                    eye, src[b * BLK : (b + 1) * BLK, a * BLK : (a + 1) * BLK]
                ).astype(BF)

    loads[0].wait()
    turn(xh, xht)
    loads[2].wait()
    turn(m, mt)
    loads[1].wait()
    loads[3].wait()

    peers = 4 + jnp.where(has_left, 1, 0) + jnp.where(has_right, 1, 0)
    pl.semaphore_wait(barrier, peers)

    quarter = dx_ref.shape[0] // 4
    me = flip + 2 * unit

    def member(o):
        p = group(o)
        return p["dir"] + 2 * p["unit"]

    def share(o):
        return pltpu.make_async_remote_copy(
            dx_ref.at[pl.ds(member(o) * quarter, quarter)],
            rx.at[o - 1],
            g_send.at[0, o - 1],
            g_recv.at[0, o - 1],
            device_id=group(o),
            device_id_type=MESH,
        )

    def spread(o):
        return pltpu.make_async_remote_copy(
            red,
            ig_ref.at[pl.ds(me * quarter, quarter)],
            g_send.at[1, o - 1],
            g_recv.at[1, o - 1],
            device_id=group(o),
            device_id_type=MESH,
        )

    for o in (1, 2, 3):
        share(o).start()

    def remote(src, dst, send, recv, k, device):
        return pltpu.make_async_remote_copy(
            src, dst, send.at[k], recv.at[k], device_id=device, device_id_type=MESH
        )

    def reduce(k, value, own_k, left_k, right_k, res_k):
        go_right = remote(own_k, left_k, r_send, l_recv, k, r_dev)
        go_left = remote(own_k, right_k, l_send, r_recv, k, l_dev)
        left_in = remote(own_k, left_k, r_send, l_recv, k, l_dev)
        right_in = remote(own_k, right_k, l_send, r_recv, k, r_dev)

        @pl.when(before)
        def _():
            @pl.when(has_left)
            def _():
                left_in.wait_recv()
                own_k[...] = (value() + left_k[...].astype(F32)).astype(BF)

            @pl.when(jnp.logical_not(has_left))
            def _():
                own_k[...] = value().astype(BF)

            go_right.start()

        @pl.when(after)
        def _():
            @pl.when(has_right)
            def _():
                right_in.wait_recv()
                own_k[...] = (value() + right_k[...].astype(F32)).astype(BF)

            @pl.when(jnp.logical_not(has_right))
            def _():
                own_k[...] = value().astype(BF)

            go_left.start()

        @pl.when(middle)
        def _():
            total = value()
            if mid > 0:
                left_in.wait_recv()
                total = total + left_k[...].astype(F32)
            if mid < lanes - 1:
                right_in.wait_recv()
                total = total + right_k[...].astype(F32)
            own_k[...] = total.astype(BF)
            if mid > 0:
                remote(own_k, res_k, l_send, r_recv, k, l_dev).start()
            if mid < lanes - 1:
                remote(own_k, res_k, r_send, l_recv, k, r_dev).start()
            remote(own_k, res_k, y_send, y_recv, k, y_dev).start()
            pltpu.make_async_copy(own_k, res_k, o_sem.at[k]).start()

    def publish(k, res_k):
        @pl.when(before)
        def _():
            remote(res_k, res_k, l_send, r_recv, k, l_dev).wait_recv()

            @pl.when(has_left)
            def _():
                remote(res_k, res_k, l_send, r_recv, k, l_dev).start()

            remote(res_k, res_k, y_send, y_recv, k, y_dev).start()

        @pl.when(after)
        def _():
            remote(res_k, res_k, r_send, l_recv, k, r_dev).wait_recv()

            @pl.when(has_right)
            def _():
                remote(res_k, res_k, r_send, l_recv, k, r_dev).start()

            remote(res_k, res_k, y_send, y_recv, k, y_dev).start()

    def finish(k, own_k, res_k):
        remote(res_k, res_k, y_send, y_recv, k, y_dev).wait()
        to_left = remote(own_k, res_k, l_send, r_recv, k, l_dev)
        to_right = remote(own_k, res_k, r_send, l_recv, k, r_dev)

        @pl.when(has_left)
        def _():
            to_left.wait_send()

        @pl.when(has_right)
        def _():
            to_right.wait_send()

        @pl.when(middle)
        def _():
            pltpu.make_async_copy(own_k, res_k, o_sem.at[k]).wait()

    ones = jnp.ones((16, rows), BF)
    total = jnp.zeros((16, BLK), F32)
    which = lax.broadcasted_iota(jnp.int32, (16, BLK), 0)
    for b in range(col_blocks):
        sums = mm(ones, dz[:, b * BLK : (b + 1) * BLK])
        total = total + jnp.where(which == b, sums, 0.0)
    acc[0:16, :] = total
    reduce(n_all, lambda: acc[0:16, :], bown, bleft, bright, bres.at[mine])

    lag = 5 * jnp.where(before, mid - lane, lane - mid) + 2

    def body(k, carry):
        @pl.when(k < n_all)
        def _():
            @pl.when(k < n_cat)
            def _():
                r = pl.multiple_of(lax.rem(k, row_blocks) * BLK, BLK)
                b = pl.multiple_of(lax.div(k, row_blocks) * BLK, BLK)
                acc[...] = mm(xht[pl.ds(r, BLK), :], dz[:, pl.ds(b, BLK)])

            @pl.when(k >= n_cat)
            def _():
                n = k - n_cat
                r = pl.multiple_of(lax.div(n, proj_cols) * BLK, BLK)
                b = pl.multiple_of(lax.rem(n, proj_cols) * BLK, BLK)
                acc[...] = mm(mt[pl.ds(r, BLK), :], dr[:, pl.ds(b, BLK)])

            reduce(
                k,
                lambda: acc[...],
                own.at[k],
                from_left.at[k],
                from_right.at[k],
                res.at[mine, k],
            )

        @pl.when(k == 10)
        def _():
            sums = dx_ref[pl.ds(me * quarter, quarter)].astype(F32)
            for o in (1, 2, 3):
                share(o).wait_recv()
                sums = sums + rx[o - 1].astype(F32)
            red[...] = sums.astype(BF)
            ig_ref[pl.ds(me * quarter, quarter)] = red[...]
            for o in (1, 2, 3):
                spread(o).start()

        n = k - lag

        @pl.when(jnp.logical_and(n >= 0, n < n_all))
        def _():
            publish(n, res.at[mine, n])

        return carry

    lax.fori_loop(0, n_all + 5 * max(mid, lanes - 1 - mid) + 2, body, 0)
    publish(n_all, bres.at[mine])

    def end(k, carry):
        finish(k, own.at[k], res.at[mine, k])
        return carry

    lax.fori_loop(0, n_all, end, 0)
    finish(n_all, bown, bres.at[mine])
    for o in (1, 2, 3):
        share(o).wait_send()
        spread(o).wait()


def gradients(lanes, dzg, xhg, mg, drg, dx):
    rows, cols = dzg.shape
    depth = xhg.shape[1]
    n_all = (depth // BLK) * (cols // BLK) + (mg.shape[1] // BLK) * (drg.shape[1] // BLK)
    steps, streams, width = dx.shape
    vmem = pl.BlockSpec(memory_space=pltpu.VMEM)
    hbm = pl.BlockSpec(memory_space=pl.ANY)
    shape = jax.ShapeDtypeStruct
    sems = pltpu.SemaphoreType.DMA((n_all + 1,))
    return pl.pallas_call(
        functools.partial(gradient_kernel, lanes),
        out_shape=(
            shape((2, n_all, BLK, BLK), BF),
            shape((2, 16, BLK), BF),
            shape((steps, streams, width), BF),
        ),
        in_specs=[hbm] * 4 + [vmem],
        out_specs=(hbm, hbm, vmem),
        scratch_shapes=[
            pltpu.VMEM((rows, cols), BF),
            pltpu.VMEM((rows, depth), BF),
            pltpu.VMEM((depth, rows), BF),
            pltpu.VMEM(mg.shape, BF),
            pltpu.VMEM((mg.shape[1], rows), BF),
            pltpu.VMEM(drg.shape, BF),
            pltpu.VMEM((BLK, BLK), F32),
            pltpu.VMEM((n_all, BLK, BLK), BF),
            pltpu.VMEM((n_all, BLK, BLK), BF),
            pltpu.VMEM((n_all, BLK, BLK), BF),
            pltpu.VMEM((16, BLK), BF),
            pltpu.VMEM((16, BLK), BF),
            pltpu.VMEM((16, BLK), BF),
            pltpu.VMEM((3, steps // 4, streams, width), BF),
            pltpu.VMEM((steps // 4, streams, width), BF),
            pltpu.SemaphoreType.DMA((4,)),
            sems,
            sems,
            sems,
            sems,
            sems,
            sems,
            sems,
            pltpu.SemaphoreType.DMA((2, 3)),
            pltpu.SemaphoreType.DMA((2, 3)),
        ],
        compiler_params=pltpu.CompilerParams(
            collective_id=1, has_side_effects=True, vmem_limit_bytes=VMEM_LIMIT
        ),
        name="gradients",
    )(dzg, xhg, mg, drg, dx)


def widen_kernel(n_cat, res, bres, wx_out, wh_out, b_out, wp_out, low, wide, bias, p_low, in_sem, out_sem, p_sem):
    units = wx_out.shape[2]
    row_blocks = low.shape[1]
    half = row_blocks // 2
    col_blocks = n_cat // row_blocks
    count = 2 * col_blocks
    n_proj = p_low.shape[1]
    proj_cols = wp_out.shape[1] // BLK

    def fetch(k, slot):
        return pltpu.make_async_copy(
            res.at[lax.div(k, col_blocks), pl.ds(lax.rem(k, col_blocks) * row_blocks, row_blocks)],
            low.at[slot],
            in_sem.at[slot],
        )

    def store(k, slot):
        owner = lax.div(k, col_blocks)
        b = lax.rem(k, col_blocks)
        gate = lax.rem(b, 4)
        u = pl.multiple_of(owner * (units // 2) + lax.div(b, 4) * BLK, BLK)
        return [
            pltpu.make_async_copy(
                wide.at[slot, i],
                out.at[:, gate, pl.ds(u, BLK)],
                out_sem.at[slot, i],
            )
            for i, out in enumerate((wx_out, wh_out))
        ]

    proj = [
        pltpu.make_async_copy(res.at[o, pl.ds(n_cat, n_proj)], p_low.at[o], p_sem.at[o])
        for o in range(2)
    ]
    for one in proj:
        one.start()
    fetch(0, 0).start()

    def body(k, carry):
        slot = lax.rem(k, 2)

        @pl.when(k + 1 < count)
        def _():
            fetch(k + 1, 1 - slot).start()

        @pl.when(k >= 2)
        def _():
            for one in store(k - 2, slot):
                one.wait()

        fetch(k, slot).wait()
        for r in range(row_blocks):
            wide[slot, r // half, (r % half) * BLK : (r % half + 1) * BLK, :] = low[slot, r].astype(F32)
        for one in store(k, slot):
            one.start()
        return carry

    lax.fori_loop(0, count, body, 0)
    for owner in range(2):
        proj[owner].wait()
        for n in range(n_proj):
            r = owner * (units // 2) + (n // proj_cols) * BLK
            col = (n % proj_cols) * BLK
            wp_out[r : r + BLK, col : col + BLK] = p_low[owner, n].astype(F32)
        for b in range(col_blocks):
            u = owner * (units // 2) + (b // 4) * BLK
            b_out[b % 4 : b % 4 + 1, u : u + BLK] = bres[owner, b : b + 1, :].astype(F32)
    for k in (count - 2, count - 1):
        for one in store(k, k % 2):
            one.wait()


def widen(res, bres, width, units):
    row_blocks = 2 * width // BLK
    n_cat = row_blocks * (2 * units // BLK)
    n_proj = res.shape[1] - n_cat
    vmem = pl.BlockSpec(memory_space=pltpu.VMEM)
    hbm = pl.BlockSpec(memory_space=pl.ANY)
    shape = jax.ShapeDtypeStruct
    return pl.pallas_call(
        functools.partial(widen_kernel, n_cat),
        out_shape=(
            shape((width, 4, units), F32),
            shape((width, 4, units), F32),
            shape((4, units), F32),
            shape((units, width), F32),
        ),
        in_specs=[hbm, vmem],
        out_specs=(hbm, hbm, vmem, vmem),
        scratch_shapes=[
            pltpu.VMEM((2, row_blocks, BLK, BLK), BF),
            pltpu.VMEM((2, 2, width, BLK), F32),
            pltpu.VMEM((8, BLK), F32),
            pltpu.VMEM((2, n_proj, BLK, BLK), BF),
            pltpu.SemaphoreType.DMA((2,)),
            pltpu.SemaphoreType.DMA((2, 2)),
            pltpu.SemaphoreType.DMA((2,)),
        ],
        compiler_params=pltpu.CompilerParams(vmem_limit_bytes=VMEM_LIMIT),
        name="widen",
    )(res, bres)


def on_device(
    inputs,
    win_count,
    last_live,
    hidden_init,
    cell_init,
    w_input,
    w_hidden,
    gate_bias,
    w_proj,
    out_grad,
):
    streams, steps, width = inputs.shape
    units = w_proj.shape[1]
    lanes = lax.axis_size("batch") // 2
    x_time = jnp.swapaxes(inputs, 0, 1)
    y_time = jnp.swapaxes(out_grad[0], 0, 1)
    lens = jnp.broadcast_to(((win_count - 1) * WIN + last_live)[:, None], (streams, 128))
    lay, hfin, cfin, dx, dzg, xhg, mg, drg = recurrence(
        x_time,
        y_time,
        lens,
        hidden_init[0],
        cell_init[0],
        gate_bias[0],
        w_input[0],
        w_hidden[0],
        w_proj[0],
    )
    rows = 2 * steps * streams
    res, bres, ig = gradients(
        lanes,
        dzg.reshape(rows, 2 * units),
        xhg.reshape(rows, 2 * width),
        mg.reshape(rows, units // 2),
        drg.reshape(rows, width),
        dx,
    )
    wx_grad, wh_grad, b_grad, wp_grad = widen(res, bres, width, units)
    return (
        jnp.swapaxes(lay, 0, 1)[None],
        jnp.swapaxes(ig, 0, 1).astype(F32),
        wx_grad[None],
        wh_grad[None],
        b_grad[None],
        wp_grad[None],
        hfin[None],
        cfin[None],
    )


def solution(mesh):
    placed = (
        P("batch", None, None),
        P("batch"),
        P("batch"),
        P("dir", "batch", None),
        P("dir", "batch", "unit"),
        P("dir", None, None, "unit"),
        P("dir", None, None, "unit"),
        P("dir", None, "unit"),
        P("dir", "unit", None),
        P("dir", "batch", None, None),
    )
    return jax.shard_map(
        on_device,
        mesh=mesh,
        in_specs=placed,
        out_specs=(
            P("dir", "batch", None, None),
            P("batch", None, None),
            P("dir", None, None, "unit"),
            P("dir", None, None, "unit"),
            P("dir", None, "unit"),
            P("dir", "unit", None),
            P("dir", "batch", None),
            P("dir", "batch", "unit"),
        ),
        check_vma=False,
    )
```

time: 2650 us -> 485 us (0.18); the launches traced: 2620 us -> 484 us
  matrix products: 1040 us -> 0 us
  local copies, waits for them, and re-layouts: 567 us -> 8.95 us
  Pallas kernels: 0 us -> 474 us
  waiting for transfers between devices: 412 us -> 0 us
  other arithmetic: 229 us -> 0.8 us
  blocking collectives: 180 us -> 0 us
  starting transfers between devices: 163 us -> 0 us
    dot_general x130 -> x0, matrix products: 1040 us -> none  [the longest x16 371 us: retreat(): lax.dot_general(joined, gate_grad, (((0,), (0,)), ((), ())), preferred_el...]
    pallas_call x0 -> x3, Pallas kernels: none -> 474 us  [the longest x1 242 us: gradients(): pl.pallas_call(functools.partial(gradient_kernel, lanes), out_shape=(shap...]
    psum x2 -> x0, waiting for transfers between devices: 333 us -> none  [the longest x1 333 us: on_device(): lax.psum(total_cat.astype(jnp.bfloat16), 'batch').astype(jnp.float32)]
    dynamic_update_slice x112 -> x0, local copies, waits for them, and re-layouts: 236 us -> none  [the longest x96 223 us: window_forward(): return lax.scan(advance, start_state, (input_block, mask_block))]
    all_to_all x48 -> x0, starting transfers between devices: 162 us -> none  [the longest x32 108 us: project(): lax.all_to_all(cell_low, 'unit', split_axis=0, concat_axis=1, tiled=True)]
    all_gather x32 -> x0, blocking collectives: 142 us -> none  [project(): hidden_all = lax.all_gather(hidden_mine, 'unit', axis=0, tiled=True)]
    another operation x28 -> x0, local copies, waits for them, and re-layouts: 87 us -> none
    all_to_all x48 -> x0, waiting for transfers between devices: 71.6 us -> none  [the longest x32 71.5 us: project(): lax.all_to_all(cell_low, 'unit', split_axis=0, concat_axis=1, tiled=True)]
  transfers between devices with their start and end apart: 68 -> 0, of which waited for: 19 -> 0; matrix products, arithmetic and copies ran while one was open for 41% -> 0% of each run, Pallas kernels for 0% -> 0%
where the time goes in v1:
time: 485 us; the launch traced here: 484 us
  Pallas kernels  474 us (98%)
  local copies, waits for them, and re-layouts  8.95 us (2%)
    pallas_call x1, Pallas kernels, gradients(): pl.pallas_call(functools.partial(gradient_kernel, lanes), out_shape=(shap...  242 us
    pallas_call x1, Pallas kernels, recurrence(): pl.pallas_call(recurrence_kernel, out_shape=(shape((steps, streams, width...  202 us
    pallas_call x1, Pallas kernels, widen(): pl.pallas_call(functools.partial(widen_kernel, n_cat), out_shape=(shape((...  29.2 us

profile of v1, /device:TPU:0, one launch (start us, length us, event | category | flops | bytes accessed | tf_op | source)
XLA Modules:
  0.0 484.1 jit_solution(8624431537693539458)
XLA Ops:
  0.6 2.1 copy.24
  2.8 2.1 copy.25
  4.9 0.7 multiply_add_fusion
  5.6 0.7 broadcast_in_dim.27.len_ref
  6.2 201.9 %recurrence.1 = (bf16[16,32,512]{2,1,0:T(8,128)(2,1)}, f32[32,512]{1,0:T(8,128)}, f32[32,2048]{1,0:T(8,128)}, bf16[16,32,512]{2,1,0:T(8,128)(2,1)}, bf16[2,16,32...) custom-call(bf16[16,32,512]{2,1,0:T(8,128)(2,1)} %bitcast.36, ...), custom_call_target="tpu_custom_call" | custom-call | tf_op jit(solution)/shard_map/recurrence/pallas_call | solution.py:384
  208.1 242.5 %gradients.1 = (bf16[2,72,256,256]{3,2,1,0:T(8,128)(2,1)}, bf16[2,16,256]{2,1,0:T(8,128)(2,1)}, bf16[16,32,512]{2,1,0:T(8,128)(2,1)}) custom-call(bf16[1024,4096]{1,0:T(8,128)(2,1)} %bitcast.29, bf16[1024,1024]{1,0:T(8,128)(2,1)} %bitcast.33, bf16[1024,1024]{1,0:T(8,128)(2,1)} %bitcast.34, bf16[1024,512]{1,0:T(8,128)(2,1)} %bitcast.37, ...), custom_call_target="tpu_custom_call" | custom-call | tf_op jit(solution)/shard_map/gradients/pallas_call | solution.py:735
  450.6 0.0 copy-start
  450.6 0.0 copy-start.1
  450.7 0.0 copy-start.3
  450.7 0.0 copy-start.2
  450.7 29.2 %widen.1 = (f32[512,4,2048]{2,1,0:T(4,128)}, f32[512,4,2048]{2,1,0:T(4,128)}, f32[4,2048]{1,0:T(4,128)}, f32[2048,512]{1,0:T(8,128)}) custom-call(bf16[2,72,256,256]{3,2,1,0:T(8,128)(2,1)} %get-tuple-element.30.res, bf16[2,16,256]{2,1,0:T(8,128)(2,1)} %get-tuple-element.31.bres), custom_call_target="tpu_custom_call" | custom-call | tf_op jit(solution)/shard_map/widen/pallas_call | solution.py:857
  479.9 0.0 copy-done
  479.9 0.1 convert_bitcast_fusion
  480.1 1.6 copy.21
  481.6 0.0 copy-done.1
  481.6 1.1 copy.20
  482.7 0.0 copy-done.3
  482.7 0.6 copy.28
  483.4 0.0 copy-done.2
  483.4 0.7 copy.29
Async XLA Ops:
  450.6 29.3 %copy-start = (bf16[16,32,512]{2,1,0:T(8,128)(2,1)S(1)}, bf16[16,32,512]{2,1,0:T(8,128)(2,1)}, u32[]{:S(2)}) copy-start(bf16[16,32,512]{2,1,0:T(8,128)(2,1)} %get-tuple-element.29) | copy-start | bytes 1572868
  450.6 31.0 %copy-start.1 = (bf16[16,32,512]{2,1,0:T(8,128)(2,1)S(1)}, bf16[16,32,512]{2,1,0:T(8,128)(2,1)}, u32[]{:S(2)}) copy-start(bf16[16,32,512]{2,1,0:T(8,128)(2,1)} %get-tuple-element.23) | copy-start | bytes 1572868
  450.7 32.1 %copy-start.3 = (f32[32,512]{1,0:T(8,128)S(1)}, f32[32,512]{1,0:T(8,128)}, u32[]{:S(2)}) copy-start(f32[32,512]{1,0:T(8,128)} %get-tuple-element.36) | copy-start | bytes 196612
  450.7 32.7 %copy-start.2 = (f32[32,2048]{1,0:T(8,128)S(1)}, f32[32,2048]{1,0:T(8,128)}, u32[]{:S(2)}) copy-start(f32[32,2048]{1,0:T(8,128)} %get-tuple-element.37) | copy-start | bytes 786436

commit v2 on v1

v2 whole, which is shorter than its diff:
```python
import functools

import jax
import jax.numpy as jnp
from jax import lax
from jax.experimental import pallas as pl
from jax.experimental.pallas import tpu as pltpu
from jax.sharding import PartitionSpec as P

WIN = 8
BLK = 256
CUT = 128
RING = 4
LAG = 8
MESH = pl.DeviceIdType.MESH
BF = jnp.bfloat16
F32 = jnp.float32
NT = (((1,), (1,)), ((), ()))
VMEM_LIMIT = 60 * 1024 * 1024
THIRD = 1.0 / 3.0


def sigmoid(v):
    return 0.5 * jnp.tanh(0.5 * v) + 0.5


def mm(a, b):
    return jnp.dot(a, b, preferred_element_type=F32)


def mm_nt(a, b):
    return lax.dot_general(a, b, NT, preferred_element_type=F32)


def identity():
    rows = lax.broadcasted_iota(jnp.int32, (BLK, BLK), 0)
    cols = lax.broadcasted_iota(jnp.int32, (BLK, BLK), 1)
    return jnp.where(rows == cols, 1.0, 0.0).astype(BF)


def gate_order():
    rows = lax.broadcasted_iota(jnp.int32, (BLK, BLK), 0)
    cols = lax.broadcasted_iota(jnp.int32, (BLK, BLK), 1)
    want = (rows & (BLK // 4 - 1)) * 4 + (rows >> 6)
    return jnp.where(want == cols, 1.0, 0.0).astype(BF)


def recurrence_kernel(
    x_hbm,
    y_hbm,
    win_ref,
    last_ref,
    h0_ref,
    c0_ref,
    bias_ref,
    wx_hbm,
    wh_hbm,
    wp_hbm,
    lay_ref,
    hfin_ref,
    cfin_ref,
    dx_ref,
    dzg,
    xhg,
    mg,
    drg,
    w,
    wht,
    wp,
    wpt,
    raw,
    z,
    c,
    th,
    x_flat,
    y_flat,
    xh,
    y_now,
    m,
    dr,
    dz,
    dc,
    dh,
    lens,
    snd,
    rcv,
    raw_sem,
    load_sem,
    ex_send,
    ex_recv,
    y_send,
    y_recv,
    own_sem,
):
    steps, streams, width = lay_ref.shape
    units = wp.shape[0]
    tiles = units // BLK
    gate4 = 4 * BLK
    half_cols = 2 * units
    half_units = units // 2
    flip = lax.axis_index("dir")
    batch = lax.axis_index("batch")
    unit = lax.axis_index("unit")
    mine = lax.rem(batch, 2)
    other = 1 - mine
    y_dev = {"batch": batch + 1 - 2 * mine}
    x_dev = {"unit": 1 - unit}
    hid = slice(width, 2 * width)

    def place(t):
        return t + flip * (steps - 1 - 2 * t)

    slots = raw.shape[0]
    span = raw.shape[2]
    halves = units // span
    blocks = halves * width * 4 // BLK

    def fetch(n, w_hbm, slot):
        b = lax.div(n, halves)
        col = lax.rem(n, halves)
        return pltpu.make_async_copy(
            w_hbm.reshape(width * 4, units).at[
                pl.ds(pl.multiple_of(b * BLK, BLK), BLK), pl.ds(pl.multiple_of(col * span, span), span)
            ],
            raw.at[slot],
            raw_sem.at[slot],
        )

    def fetch_any(n):
        slot = lax.rem(n, slots)

        @pl.when(n < blocks)
        def _():
            fetch(n, wx_hbm, slot).start()

        @pl.when(jnp.logical_and(n >= blocks, n < 2 * blocks))
        def _():
            fetch(n - blocks, wh_hbm, slot).start()

    for n in range(slots - 1):
        fetch(n, wx_hbm, n).start()
    x_copy = pltpu.make_async_copy(x_hbm.reshape(streams * steps, width), x_flat, load_sem.at[0])
    y_copy = pltpu.make_async_copy(y_hbm.reshape(streams * steps, width), y_flat, load_sem.at[1])
    proj_copy = pltpu.make_async_copy(wp_hbm, wp, load_sem.at[2])
    x_copy.start()
    proj_copy.start()
    y_copy.start()
    barrier = pltpu.get_barrier_semaphore()
    pl.semaphore_signal(barrier, 1, device_id=x_dev, device_id_type=MESH)
    pl.semaphore_signal(barrier, 1, device_id=y_dev, device_id_type=MESH)

    order = gate_order()

    def spread(n, carry):
        slot = lax.rem(n, slots)
        fetch_any(n + slots - 1)
        fetch(0, wx_hbm, slot).wait()
        which = lax.div(n, blocks)
        left = n - which * blocks
        row = pl.multiple_of(lax.div(left, halves) * 64, 64)
        col = lax.rem(left, halves) * (4 * span)
        for j in range(span // BLK):
            got = mm(order, raw[slot, :, j * BLK : (j + 1) * BLK]).astype(BF)
            for g in range(4):
                w[
                    which,
                    pl.ds(row, 64),
                    pl.ds(pl.multiple_of(col + j * gate4 + g * BLK, BLK), BLK),
                ] = got[g * 64 : (g + 1) * 64]
        return carry

    lax.fori_loop(0, 2 * blocks, spread, 0)
    wx, wh = w.at[0], w.at[1]

    row_len = ((win_ref[...] - 1) * WIN + last_ref[...]).astype(F32)
    rows = lax.broadcasted_iota(jnp.int32, (streams, streams), 0)
    cols = lax.broadcasted_iota(jnp.int32, (streams, streams), 1)
    spot = jnp.where(rows == cols, jnp.broadcast_to(row_len, (streams, streams)), 0.0)
    lens[...] = jnp.broadcast_to(jnp.sum(spot, axis=1, keepdims=True), lens.shape)

    def live_of(t, count):
        live = jnp.where(lens[...] > place(t).astype(F32), 1.0, 0.0)
        return jnp.concatenate([live] * (count // 128), 1)

    def pick(flat, t):
        s = lax.broadcasted_iota(jnp.int32, (streams, streams * steps), 0)
        r = lax.broadcasted_iota(jnp.int32, (streams, streams * steps), 1)
        want = jnp.where(r == s * steps + place(t), 1.0, 0.0).astype(BF)
        return mm(want, flat[...]).astype(BF)

    def exchange(k):
        slot = lax.rem(k, 2)
        return pltpu.make_async_remote_copy(
            snd.at[slot],
            rcv.at[slot],
            ex_send.at[slot],
            ex_recv.at[slot],
            device_id=x_dev,
            device_id_type=MESH,
        )

    def pair(kind, t, away, keep, target):
        return (
            pltpu.make_async_remote_copy(
                away,
                target,
                y_send.at[kind, t],
                y_recv.at[kind, t],
                device_id=y_dev,
                device_id_type=MESH,
            ),
            pltpu.make_async_copy(keep, target, own_sem.at[kind, t]),
        )

    def xh_pair(t):
        return pair(0, t, xh.at[t], xh.at[t], xhg.at[mine, place(t)])

    def m_pair(t):
        slot = lax.rem(t, RING)
        away = m.at[slot, :, pl.ds(pl.multiple_of(other * half_units, half_units), half_units)]
        keep = m.at[slot, :, pl.ds(pl.multiple_of(mine * half_units, half_units), half_units)]
        return pair(1, t, away, keep, mg.at[mine, place(t)])

    def dr_pair(t):
        return pair(2, t, dr.at[t], dr.at[t], drg.at[mine, place(t)])

    def dz_pair(t):
        slot = lax.rem(t, RING)
        away = dz.at[slot, :, pl.ds(pl.multiple_of(other * half_cols, half_cols), half_cols)]
        keep = dz.at[slot, :, pl.ds(pl.multiple_of(mine * half_cols, half_cols), half_cols)]
        return pair(3, t, away, keep, dzg.at[mine, place(t)])

    def begin(copies):
        for one in copies:
            one.start()

    def sent(copies):
        copies[0].wait_send()
        copies[1].wait()

    def input_part(t):
        now = xh[t, :, :width]
        for j in range(tiles):
            part = mm(now, wx[:, j * gate4 : (j + 1) * gate4])
            for g in range(4):
                z[t, :, j * gate4 + g * BLK : j * gate4 + (g + 1) * BLK] = (
                    part[:, g * BLK : (g + 1) * BLK] + bias_ref[g : g + 1, j * BLK : (j + 1) * BLK]
                )

    eye = identity()
    x_copy.wait()
    xh[0, :, :width] = pick(x_flat, 0)
    xh[0, :, hid] = h0_ref[...].astype(BF)
    c[0] = c0_ref[...]
    input_part(0)
    proj_copy.wait()
    y_copy.wait()
    turn_cols = 4 * units // steps
    turn_units = units // steps
    pl.semaphore_wait(barrier, 2)

    def forward(t, carry):
        slot = lax.rem(t, RING)

        @pl.when(t >= RING)
        def _():
            sent(m_pair(t - RING))

        live = live_of(t, BLK) > 0.5
        hidden = xh[t, :, hid]
        for j in range(tiles):
            cols = slice(j * BLK, (j + 1) * BLK)
            base = j * gate4
            pre = z[t, :, base : base + gate4] + mm(hidden, wh[:, base : base + gate4])
            in_gate = sigmoid(pre[:, :BLK])
            forget = sigmoid(pre[:, BLK : 2 * BLK])
            cand = jnp.tanh(pre[:, 2 * BLK : 3 * BLK])
            out_gate = sigmoid(pre[:, 3 * BLK :])
            prev = c[t, :, cols]
            new = 3.0 * jnp.tanh((forget * prev + in_gate * cand) * THIRD)
            m[slot, :, cols] = (out_gate * jnp.tanh(new)).astype(BF)
            z[t, :, base : base + BLK] = in_gate
            z[t, :, base + BLK : base + 2 * BLK] = forget
            z[t, :, base + 2 * BLK : base + 3 * BLK] = cand
            z[t, :, base + 3 * BLK : base + gate4] = out_gate
            c[t + 1, :, cols] = jnp.where(live, new, prev)
        two = lax.rem(t, 2)
        snd[two] = mm(m[slot], wp[...]).astype(BF)
        copy = exchange(t)
        copy.start()
        begin(xh_pair(t))
        begin(m_pair(t))

        @pl.when(t + 1 < steps)
        def _():
            xh[t + 1, :, :width] = pick(x_flat, t + 1)
            input_part(t + 1)

        at = pl.multiple_of(t * turn_cols, turn_cols)
        for kb in range(width // BLK):
            for cb in range(turn_cols // BLK):
                wht[pl.ds(at + cb * BLK, BLK), kb * BLK : (kb + 1) * BLK] = mm_nt(
                    eye, wh[kb * BLK : (kb + 1) * BLK, pl.ds(at + cb * BLK, BLK)]
                ).astype(BF)
        at = pl.multiple_of(t * turn_units, turn_units)
        for kb in range(width // BLK):
            wpt[kb * BLK : (kb + 1) * BLK, pl.ds(at, turn_units)] = mm_nt(
                eye, wp[pl.ds(at, turn_units), kb * BLK : (kb + 1) * BLK]
            ).astype(BF)
        copy.wait()
        total = snd[two].astype(F32) + rcv[two].astype(F32)
        squash = jnp.tanh(total * THIRD)
        th[t] = squash
        new_hidden = (3.0 * squash).astype(BF).astype(F32)
        live_h = live_of(t, width)
        lay_ref[place(t)] = (xh[t, :, :width].astype(F32) + live_h * new_hidden).astype(BF)
        after = jnp.where(live_h > 0.5, new_hidden, hidden.astype(F32))

        @pl.when(t + 1 < steps)
        def _():
            xh[t + 1, :, hid] = after.astype(BF)

        @pl.when(t + 1 == steps)
        def _():
            hfin_ref[...] = after

        return carry

    lax.fori_loop(0, steps, forward, 0)
    cfin_ref[...] = c[steps]
    dc[...] = jnp.zeros_like(dc)
    dh[...] = jnp.zeros_like(dh)
    y_now[0] = pick(y_flat, steps - 1)

    def backward(k, carry):
        t = steps - 1 - k
        slot = lax.rem(t, RING)
        two = lax.rem(k, 2)

        @pl.when(k >= RING)
        def _():
            sent(dz_pair(t + RING))

        grad_hidden = dh[...]
        live_h = live_of(t, width)
        squash = th[t]
        y_low = y_now[two].astype(F32)
        low = (live_h * (y_low + grad_hidden) * (1.0 - squash * squash)).astype(BF)
        dr[t] = low
        live = live_of(t, BLK)
        part = jnp.zeros((streams, width), F32)
        for j in range(tiles):
            cols = slice(j * BLK, (j + 1) * BLK)
            base = j * gate4
            grad_m = mm(low, wpt[:, cols]).astype(BF).astype(F32)
            in_gate = z[t, :, base : base + BLK]
            forget = z[t, :, base + BLK : base + 2 * BLK]
            cand = z[t, :, base + 2 * BLK : base + 3 * BLK]
            out_gate = z[t, :, base + 3 * BLK : base + gate4]
            prev = c[t, :, cols]
            new = c[t + 1, :, cols]
            grad_c = dc[:, cols]
            tanh_new = jnp.tanh(new)
            grad_n = live * grad_c + grad_m * out_gate * (1.0 - tanh_new * tanh_new)
            third = new * THIRD
            grad_u = grad_n * (1.0 - third * third)
            dz[slot, :, base : base + BLK] = (grad_u * cand * in_gate * (1.0 - in_gate)).astype(BF)
            dz[slot, :, base + BLK : base + 2 * BLK] = (
                grad_u * prev * forget * (1.0 - forget)
            ).astype(BF)
            dz[slot, :, base + 2 * BLK : base + 3 * BLK] = (
                grad_u * in_gate * (1.0 - cand * cand)
            ).astype(BF)
            dz[slot, :, base + 3 * BLK : base + gate4] = (
                grad_m * tanh_new * out_gate * (1.0 - out_gate)
            ).astype(BF)
            dc[:, cols] = (1.0 - live) * grad_c + grad_u * forget
            part = part + mm(dz[slot, :, base : base + gate4], wht[base : base + gate4, :])
        snd[two] = part.astype(BF)
        copy = exchange(k)
        copy.start()
        begin(dz_pair(t))
        begin(dr_pair(t))

        @pl.when(k + 1 < steps)
        def _():
            y_now[1 - two] = pick(y_flat, t - 1)

        grad_x = y_low * jnp.where(unit == 0, 1.0, 0.0)
        for j in range(tiles):
            base = j * gate4
            grad_x = grad_x + mm_nt(dz[slot, :, base : base + gate4], wx[:, base : base + gate4])
        dx_ref[place(t)] = grad_x.astype(BF)
        copy.wait()
        dh[...] = (1.0 - live_h) * grad_hidden + (snd[two].astype(F32) + rcv[two].astype(F32))
        return carry

    lax.fori_loop(0, steps, backward, 0)

    def last(i, carry):
        sent(m_pair(steps - RING + i))
        sent(dz_pair(i))
        return carry

    lax.fori_loop(0, RING, last, 0)

    def finish(t, carry):
        sent(xh_pair(t))
        sent(dr_pair(t))
        xh_pair(t)[0].wait_recv()
        m_pair(t)[0].wait_recv()
        dr_pair(t)[0].wait_recv()
        dz_pair(t)[0].wait_recv()
        return carry

    lax.fori_loop(0, steps, finish, 0)


def recurrence(inputs, out_grad, win, last, hidden0, cell0, bias, w_in, w_hid, proj):
    streams, steps, width = inputs.shape
    units = proj.shape[0]
    vmem = pl.BlockSpec(memory_space=pltpu.VMEM)
    hbm = pl.BlockSpec(memory_space=pl.ANY)
    shape = jax.ShapeDtypeStruct
    return pl.pallas_call(
        recurrence_kernel,
        out_shape=(
            shape((steps, streams, width), BF),
            shape((streams, width), F32),
            shape((streams, units), F32),
            shape((steps, streams, width), BF),
            shape((2, steps, streams, 2 * units), BF),
            shape((2, steps, streams, 2 * width), BF),
            shape((2, steps, streams, units // 2), BF),
            shape((2, steps, streams, width), BF),
        ),
        in_specs=[hbm] * 2 + [vmem] * 5 + [hbm] * 3,
        out_specs=(vmem, vmem, vmem, vmem, hbm, hbm, hbm, hbm),
        scratch_shapes=[
            pltpu.VMEM((2, width, 4 * units), BF),
            pltpu.VMEM((4 * units, width), BF),
            pltpu.VMEM((units, width), BF),
            pltpu.VMEM((width, units), BF),
            pltpu.VMEM((4, BLK, units // 2), BF),
            pltpu.VMEM((steps, streams, 4 * units), F32),
            pltpu.VMEM((steps + 1, streams, units), F32),
            pltpu.VMEM((steps, streams, width), F32),
            pltpu.VMEM((streams * steps, width), BF),
            pltpu.VMEM((streams * steps, width), BF),
            pltpu.VMEM((steps, streams, 2 * width), BF),
            pltpu.VMEM((2, streams, width), BF),
            pltpu.VMEM((RING, streams, units), BF),
            pltpu.VMEM((steps, streams, width), BF),
            pltpu.VMEM((RING, streams, 4 * units), BF),
            pltpu.VMEM((streams, units), F32),
            pltpu.VMEM((streams, width), F32),
            pltpu.VMEM((streams, 128), F32),
            pltpu.VMEM((2, streams, width), BF),
            pltpu.VMEM((2, streams, width), BF),
            pltpu.SemaphoreType.DMA((4,)),
            pltpu.SemaphoreType.DMA((3,)),
            pltpu.SemaphoreType.DMA((2,)),
            pltpu.SemaphoreType.DMA((2,)),
            pltpu.SemaphoreType.DMA((4, steps)),
            pltpu.SemaphoreType.DMA((4, steps)),
            pltpu.SemaphoreType.DMA((4, steps)),
        ],
        compiler_params=pltpu.CompilerParams(
            collective_id=0, has_side_effects=True, vmem_limit_bytes=VMEM_LIMIT
        ),
        name="recurrence",
    )(inputs, out_grad, win, last, hidden0, cell0, bias, w_in, w_hid, proj)


def gradient_kernel(
    lanes,
    dz_hbm,
    xh_hbm,
    m_hbm,
    dr_hbm,
    dx_ref,
    res,
    bres,
    ig_ref,
    dz,
    xh,
    xht,
    m,
    mt,
    dr,
    acc,
    bsum,
    own,
    from_left,
    from_right,
    bown,
    bleft,
    bright,
    rx,
    red,
    load_sem,
    dz_sem,
    l_recv,
    r_recv,
    y_recv,
    l_send,
    r_send,
    y_send,
    o_sem,
    g_send,
    g_recv,
):
    rows, cols = dz.shape
    depth = xh.shape[1]
    row_blocks = depth // CUT
    col_blocks = cols // BLK
    n_cat = row_blocks * col_blocks
    proj_cols = dr.shape[1] // BLK
    n_all = n_cat + (m.shape[1] // CUT) * proj_cols
    flip = lax.axis_index("dir")
    batch = lax.axis_index("batch")
    unit = lax.axis_index("unit")
    mine = lax.rem(batch, 2)
    lane = lax.div(batch, 2)
    mid = lanes // 2
    y_dev = {"batch": batch + 1 - 2 * mine}
    l_dev = {"batch": batch - 2}
    r_dev = {"batch": batch + 2}
    has_left = lane > 0
    has_right = lane < lanes - 1
    before = lane < mid
    after = lane > mid
    middle = lane == mid

    def group(o):
        return {
            "dir": flip + (o % 2) * (1 - 2 * flip),
            "unit": unit + (o // 2) * (1 - 2 * unit),
        }

    barrier = pltpu.get_barrier_semaphore()
    pl.semaphore_signal(barrier, 1, device_id=y_dev, device_id_type=MESH)
    for o in (1, 2, 3):
        pl.semaphore_signal(barrier, 1, device_id=group(o), device_id_type=MESH)

    @pl.when(has_left)
    def _():
        pl.semaphore_signal(barrier, 1, device_id=l_dev, device_id_type=MESH)

    @pl.when(has_right)
    def _():
        pl.semaphore_signal(barrier, 1, device_id=r_dev, device_id_type=MESH)

    xh_load = pltpu.make_async_copy(xh_hbm, xh, load_sem.at[0])
    m_load = pltpu.make_async_copy(m_hbm, m, load_sem.at[1])
    dr_load = pltpu.make_async_copy(dr_hbm, dr, load_sem.at[2])

    def dz_load(b):
        at = pl.ds(pl.multiple_of(b * BLK, BLK), BLK)
        return pltpu.make_async_copy(dz_hbm.at[:, at], dz.at[:, at], dz_sem.at[b])

    xh_load.start()

    def load_all(b, carry):
        dz_load(b).start()
        return carry

    lax.fori_loop(0, col_blocks, load_all, 0)
    m_load.start()
    dr_load.start()

    eye = identity()

    def turn(src, dst, a):
        at = pl.ds(pl.multiple_of(a * BLK, BLK), BLK)
        for b in range(rows // BLK):
            dst[at, b * BLK : (b + 1) * BLK] = mm_nt(
                eye, src[b * BLK : (b + 1) * BLK, at]
            ).astype(BF)

    quarter = dx_ref.shape[0] // 4
    me = flip + 2 * unit

    def member(o):
        p = group(o)
        return p["dir"] + 2 * p["unit"]

    def share(o):
        return pltpu.make_async_remote_copy(
            dx_ref.at[pl.ds(member(o) * quarter, quarter)],
            rx.at[o - 1],
            g_send.at[0, o - 1],
            g_recv.at[0, o - 1],
            device_id=group(o),
            device_id_type=MESH,
        )

    def hand_out(o):
        return pltpu.make_async_remote_copy(
            red,
            ig_ref.at[pl.ds(me * quarter, quarter)],
            g_send.at[1, o - 1],
            g_recv.at[1, o - 1],
            device_id=group(o),
            device_id_type=MESH,
        )

    bsum[...] = jnp.zeros_like(bsum)
    xh_load.wait()
    turn(xh, xht, 0)
    peers = 4 + jnp.where(has_left, 1, 0) + jnp.where(has_right, 1, 0)
    pl.semaphore_wait(barrier, peers)

    def remote(src, dst, send, recv, k, device):
        return pltpu.make_async_remote_copy(
            src, dst, send.at[k], recv.at[k], device_id=device, device_id_type=MESH
        )

    class Chunk:
        def __init__(self, k, own_k, left_k, right_k, res_k):
            self.k, self.own, self.left, self.right, self.res = k, own_k, left_k, right_k, res_k

        def to_left(self, src):
            return remote(src, self.right, l_send, r_recv, self.k, l_dev)

        def to_right(self, src):
            return remote(src, self.left, r_send, l_recv, self.k, r_dev)

        def left_in(self):
            return remote(self.own, self.left, r_send, l_recv, self.k, l_dev)

        def right_in(self):
            return remote(self.own, self.right, l_send, r_recv, self.k, r_dev)

        def to_y(self, src):
            return remote(src, self.res, y_send, y_recv, self.k, y_dev)

        def keep(self, src):
            return pltpu.make_async_copy(src, self.res, o_sem.at[self.k])

        def reduce(self, value):
            @pl.when(before)
            def _():
                @pl.when(has_left)
                def _():
                    self.left_in().wait_recv()
                    self.own[...] = (value() + self.left[...].astype(F32)).astype(BF)

                @pl.when(jnp.logical_not(has_left))
                def _():
                    self.own[...] = value().astype(BF)

                self.to_right(self.own).start()

            @pl.when(after)
            def _():
                @pl.when(has_right)
                def _():
                    self.right_in().wait_recv()
                    self.own[...] = (value() + self.right[...].astype(F32)).astype(BF)

                @pl.when(jnp.logical_not(has_right))
                def _():
                    self.own[...] = value().astype(BF)

                self.to_left(self.own).start()

            @pl.when(middle)
            def _():
                total = value()
                if mid > 0:
                    self.left_in().wait_recv()
                    total = total + self.left[...].astype(F32)
                if mid < lanes - 1:
                    self.right_in().wait_recv()
                    total = total + self.right[...].astype(F32)
                self.own[...] = total.astype(BF)
                if mid > 0:
                    self.to_left(self.own).start()
                if mid < lanes - 1:
                    self.to_right(self.own).start()
                self.to_y(self.own).start()
                self.keep(self.own).start()

        def publish(self):
            @pl.when(before)
            def _():
                self.right_in().wait_recv()

                @pl.when(has_left)
                def _():
                    self.to_left(self.right).start()

                self.to_y(self.right).start()
                self.keep(self.right).start()

            @pl.when(after)
            def _():
                self.left_in().wait_recv()

                @pl.when(has_right)
                def _():
                    self.to_right(self.left).start()

                self.to_y(self.left).start()
                self.keep(self.left).start()

        def finish(self):
            self.to_y(self.own).wait()

            @pl.when(has_left)
            def _():
                self.to_left(self.own).wait_send()

            @pl.when(has_right)
            def _():
                self.to_right(self.own).wait_send()

            self.keep(self.own).wait()

    def chunk(k):
        return Chunk(k, own.at[k], from_left.at[k], from_right.at[k], res.at[mine, k])

    bias = Chunk(n_all, bown, bleft, bright, bres.at[mine])
    ones = jnp.ones((16, rows), BF)
    which = lax.broadcasted_iota(jnp.int32, (16, BLK), 0)
    lag = LAG * jnp.where(before, mid - lane, lane - mid) + 3
    turns = depth // BLK

    def body(k, carry):
        @pl.when(jnp.logical_and(k > 0, k < turns))
        def _():
            turn(xh, xht, k)

        @pl.when(k == row_blocks)
        def _():
            m_load.wait()
            dr_load.wait()
            for o in (1, 2, 3):
                share(o).start()

        @pl.when(jnp.logical_and(k >= row_blocks, k < row_blocks + m.shape[1] // BLK))
        def _():
            turn(m, mt, k - row_blocks)

        @pl.when(k < n_all)
        def _():
            @pl.when(k < n_cat)
            def _():
                b = lax.div(k, row_blocks)
                r = pl.multiple_of(lax.rem(k, row_blocks) * CUT, CUT)
                at = pl.ds(pl.multiple_of(b * BLK, BLK), BLK)

                @pl.when(r == 0)
                def _():
                    dz_load(b).wait()
                    bsum[...] += jnp.where(which == b, mm(ones, dz[:, at]), 0.0)

                acc[...] = mm(xht[pl.ds(r, CUT), :], dz[:, at])

            @pl.when(k >= n_cat)
            def _():
                n = k - n_cat
                r = pl.multiple_of(lax.div(n, proj_cols) * CUT, CUT)
                b = pl.multiple_of(lax.rem(n, proj_cols) * BLK, BLK)
                acc[...] = mm(mt[pl.ds(r, CUT), :], dr[:, pl.ds(b, BLK)])

            chunk(k).reduce(lambda: acc[...])

            @pl.when(k == n_cat)
            def _():
                bias.reduce(lambda: bsum[...])

        @pl.when(k == 4 * row_blocks)
        def _():
            sums = dx_ref[pl.ds(me * quarter, quarter)].astype(F32)
            for o in (1, 2, 3):
                share(o).wait_recv()
                sums = sums + rx[o - 1].astype(F32)
            red[...] = sums.astype(BF)
            ig_ref[pl.ds(me * quarter, quarter)] = red[...]
            for o in (1, 2, 3):
                hand_out(o).start()

        n = k - lag

        @pl.when(jnp.logical_and(n >= 0, n < n_all))
        def _():
            chunk(n).publish()

            @pl.when(n == n_cat)
            def _():
                bias.publish()

        return carry

    lax.fori_loop(0, n_all + LAG * max(mid, lanes - 1 - mid) + 3, body, 0)

    def end(k, carry):
        chunk(k).finish()
        return carry

    lax.fori_loop(0, n_all, end, 0)
    bias.finish()
    for o in (1, 2, 3):
        share(o).wait_send()
        hand_out(o).wait()


def gradients(lanes, dzg, xhg, mg, drg, dx):
    rows, cols = dzg.shape
    depth = xhg.shape[1]
    n_all = (depth // CUT) * (cols // BLK) + (mg.shape[1] // CUT) * (drg.shape[1] // BLK)
    steps, streams, width = dx.shape
    vmem = pl.BlockSpec(memory_space=pltpu.VMEM)
    hbm = pl.BlockSpec(memory_space=pl.ANY)
    shape = jax.ShapeDtypeStruct
    sems = pltpu.SemaphoreType.DMA((n_all + 1,))
    return pl.pallas_call(
        functools.partial(gradient_kernel, lanes),
        out_shape=(
            shape((2, n_all, CUT, BLK), BF),
            shape((2, 16, BLK), BF),
            shape((steps, streams, width), BF),
        ),
        in_specs=[hbm] * 4 + [vmem],
        out_specs=(hbm, hbm, vmem),
        scratch_shapes=[
            pltpu.VMEM((rows, cols), BF),
            pltpu.VMEM((rows, depth), BF),
            pltpu.VMEM((depth, rows), BF),
            pltpu.VMEM(mg.shape, BF),
            pltpu.VMEM((mg.shape[1], rows), BF),
            pltpu.VMEM(drg.shape, BF),
            pltpu.VMEM((CUT, BLK), F32),
            pltpu.VMEM((16, BLK), F32),
            pltpu.VMEM((n_all, CUT, BLK), BF),
            pltpu.VMEM((n_all, CUT, BLK), BF),
            pltpu.VMEM((n_all, CUT, BLK), BF),
            pltpu.VMEM((16, BLK), BF),
            pltpu.VMEM((16, BLK), BF),
            pltpu.VMEM((16, BLK), BF),
            pltpu.VMEM((3, steps // 4, streams, width), BF),
            pltpu.VMEM((steps // 4, streams, width), BF),
            pltpu.SemaphoreType.DMA((3,)),
            pltpu.SemaphoreType.DMA((cols // BLK,)),
            sems,
            sems,
            sems,
            sems,
            sems,
            sems,
            sems,
            pltpu.SemaphoreType.DMA((2, 3)),
            pltpu.SemaphoreType.DMA((2, 3)),
        ],
        compiler_params=pltpu.CompilerParams(
            collective_id=1, has_side_effects=True, vmem_limit_bytes=VMEM_LIMIT
        ),
        name="gradients",
    )(dzg, xhg, mg, drg, dx)


def widen_kernel(
    n_cat,
    res,
    bres,
    lay_in,
    ig_in,
    hfin_in,
    cfin_in,
    lay_out,
    ig_out,
    wx_out,
    wh_out,
    b_out,
    wp_out,
    hfin_out,
    cfin_out,
    low,
    wide,
    lay_buf,
    ig_buf,
    p_low,
    in_sem,
    out_sem,
    p_sem,
    s_sem,
    ig_sem,
):
    width, _, units = wx_out.shape
    steps, streams, _ = lay_in.shape
    slots = low.shape[0]
    row_blocks = low.shape[1]
    half = row_blocks // 2
    col_blocks = n_cat // row_blocks
    count = 2 * col_blocks
    n_proj = p_low.shape[1]
    proj_cols = width // BLK

    def fetch(k):
        slot = lax.rem(k, slots)
        return pltpu.make_async_copy(
            res.at[lax.div(k, col_blocks), pl.ds(lax.rem(k, col_blocks) * row_blocks, row_blocks)],
            low.at[slot],
            in_sem.at[slot],
        )

    def store(k):
        slot = lax.rem(k, slots)
        owner = lax.div(k, col_blocks)
        b = lax.rem(k, col_blocks)
        gate = lax.rem(b, 4)
        u = pl.multiple_of(owner * (units // 2) + lax.div(b, 4) * BLK, BLK)
        return [
            pltpu.make_async_copy(
                wide.at[slot, i],
                out.at[:, gate, pl.ds(u, BLK)],
                out_sem.at[slot, i],
            )
            for i, out in enumerate((wx_out, wh_out))
        ]

    for k in range(slots - 1):
        fetch(k).start()
    proj = [
        pltpu.make_async_copy(res.at[o, pl.ds(n_cat, n_proj)], p_low.at[o], p_sem.at[o])
        for o in range(2)
    ]
    states = [
        pltpu.make_async_copy(hfin_in, hfin_out, s_sem.at[0]),
        pltpu.make_async_copy(cfin_in, cfin_out, s_sem.at[1]),
    ]
    for one in proj + states:
        one.start()

    def body(k, carry):
        slot = lax.rem(k, slots)

        @pl.when(k >= slots)
        def _():
            for one in store(k - slots):
                one.wait()

        fetch(k).wait()
        for r in range(row_blocks):
            wide[slot, r // half, (r % half) * CUT : (r % half + 1) * CUT, :] = low[slot, r].astype(F32)
        for one in store(k):
            one.start()

        @pl.when(k + slots - 1 < count)
        def _():
            fetch(k + slots - 1).start()

        return carry

    lax.fori_loop(0, slots, body, 0)

    t = lax.broadcasted_iota(jnp.int32, (steps, streams * steps), 0)
    r = lax.broadcasted_iota(jnp.int32, (steps, streams * steps), 1)
    flat = lay_in[...].reshape(streams * steps, width)
    bunch = BLK // steps
    for b in range(streams // bunch):
        want = jnp.concatenate(
            [jnp.where(r == t * streams + b * bunch + s, 1.0, 0.0) for s in range(bunch)], 0
        ).astype(BF)
        lay_buf[b * BLK : (b + 1) * BLK, :] = mm(want, flat).astype(BF)
    lay_copy = pltpu.make_async_copy(lay_buf, lay_out.reshape(streams * steps, width), s_sem.at[2])
    lay_copy.start()
    ig_copies = []
    for step in range(steps):
        ig_buf[step] = ig_in[step].astype(F32)
        ig_copies.append(
            pltpu.make_async_copy(ig_buf.at[step], ig_out.at[:, step, :], ig_sem.at[step])
        )
        ig_copies[-1].start()
    for owner in range(2):
        proj[owner].wait()
        for n in range(n_proj):
            row = owner * (units // 2) + (n // proj_cols) * CUT
            col = (n % proj_cols) * BLK
            wp_out[row : row + CUT, col : col + BLK] = p_low[owner, n].astype(F32)
        for b in range(col_blocks):
            u = owner * (units // 2) + (b // 4) * BLK
            b_out[b % 4 : b % 4 + 1, u : u + BLK] = bres[owner, b : b + 1, :].astype(F32)

    lax.fori_loop(slots, count, body, 0)
    for k in range(count - slots, count):
        for one in store(k):
            one.wait()
    for one in [*states, lay_copy, *ig_copies]:
        one.wait()


def widen(res, bres, lay, ig, hfin, cfin):
    steps, streams, width = lay.shape
    units = cfin.shape[1]
    row_blocks = 2 * width // CUT
    n_cat = row_blocks * (2 * units // BLK)
    n_proj = res.shape[1] - n_cat
    slots = 4
    vmem = pl.BlockSpec(memory_space=pltpu.VMEM)
    hbm = pl.BlockSpec(memory_space=pl.ANY)
    shape = jax.ShapeDtypeStruct
    return pl.pallas_call(
        functools.partial(widen_kernel, n_cat),
        out_shape=(
            shape((streams, steps, width), BF),
            shape((streams, steps, width), F32),
            shape((width, 4, units), F32),
            shape((width, 4, units), F32),
            shape((4, units), F32),
            shape((units, width), F32),
            shape((streams, width), F32),
            shape((streams, units), F32),
        ),
        in_specs=[hbm, vmem, vmem, vmem, hbm, hbm],
        out_specs=(hbm, hbm, hbm, hbm, vmem, vmem, hbm, hbm),
        scratch_shapes=[
            pltpu.VMEM((slots, row_blocks, CUT, BLK), BF),
            pltpu.VMEM((slots, 2, width, BLK), F32),
            pltpu.VMEM((streams * steps, width), BF),
            pltpu.VMEM((steps, streams, width), F32),
            pltpu.VMEM((2, n_proj, CUT, BLK), BF),
            pltpu.SemaphoreType.DMA((slots,)),
            pltpu.SemaphoreType.DMA((slots, 2)),
            pltpu.SemaphoreType.DMA((2,)),
            pltpu.SemaphoreType.DMA((3,)),
            pltpu.SemaphoreType.DMA((steps,)),
        ],
        compiler_params=pltpu.CompilerParams(vmem_limit_bytes=VMEM_LIMIT),
        name="widen",
    )(res, bres, lay, ig, hfin, cfin)


def on_device(
    inputs,
    win_count,
    last_live,
    hidden_init,
    cell_init,
    w_input,
    w_hidden,
    gate_bias,
    w_proj,
    out_grad,
):
    streams, steps, width = inputs.shape
    units = w_proj.shape[1]
    lanes = lax.axis_size("batch") // 2
    lay, hfin, cfin, dx, dzg, xhg, mg, drg = recurrence(
        inputs,
        out_grad[0],
        win_count.reshape(1, streams),
        last_live.reshape(1, streams),
        hidden_init[0],
        cell_init[0],
        gate_bias[0],
        w_input[0],
        w_hidden[0],
        w_proj[0],
    )
    rows = 2 * steps * streams
    res, bres, ig = gradients(
        lanes,
        dzg.reshape(rows, 2 * units),
        xhg.reshape(rows, 2 * width),
        mg.reshape(rows, units // 2),
        drg.reshape(rows, width),
        dx,
    )
    out = widen(res, bres, lay, ig, hfin, cfin)
    layer_out, input_grad, wx_grad, wh_grad, b_grad, wp_grad, hidden_final, cell_final = out
    return (
        layer_out[None],
        input_grad,
        wx_grad[None],
        wh_grad[None],
        b_grad[None],
        wp_grad[None],
        hidden_final[None],
        cell_final[None],
    )


def solution(mesh):
    placed = (
        P("batch", None, None),
        P("batch"),
        P("batch"),
        P("dir", "batch", None),
        P("dir", "batch", "unit"),
        P("dir", None, None, "unit"),
        P("dir", None, None, "unit"),
        P("dir", None, "unit"),
        P("dir", "unit", None),
        P("dir", "batch", None, None),
    )
    return jax.shard_map(
        on_device,
        mesh=mesh,
        in_specs=placed,
        out_specs=(
            P("dir", "batch", None, None),
            P("batch", None, None),
            P("dir", None, None, "unit"),
            P("dir", None, None, "unit"),
            P("dir", None, "unit"),
            P("dir", "unit", None),
            P("dir", "batch", None),
            P("dir", "batch", "unit"),
        ),
        check_vma=False,
    )
```

time: 485 us -> 463 us (0.955)
  Pallas kernels: 474 us -> 461 us
  local copies, waits for them, and re-layouts: 8.95 us -> 0 us
    unnamed x14 -> x0, local copies, waits for them, and re-layouts: 8.27 us -> none
    pallas_call x1, Pallas kernels: 29.2 us -> 22.1 us  [widen(): pl.pallas_call(functools.partial(widen_kernel, n_cat), out_shape=(shape((...]
where the time goes in v2:
time: 463 us; the launch traced here: 462 us
  Pallas kernels  461 us (100%)
    pallas_call x1, Pallas kernels, gradients(): pl.pallas_call(functools.partial(gradient_kernel, lanes), out_shape=(shap...  240 us
    pallas_call x1, Pallas kernels, recurrence(): pl.pallas_call(recurrence_kernel, out_shape=(shape((steps, streams, width...  200 us
    pallas_call x1, Pallas kernels, widen(): pl.pallas_call(functools.partial(widen_kernel, n_cat), out_shape=(shape((...  22.1 us

profile of v2, /device:TPU:0, one launch (start us, length us, event | category | flops | bytes accessed | tf_op | source)
XLA Modules:
  0.0 462.3 jit_solution(10403611843336328051)
XLA Ops:
  0.6 199.9 %recurrence.1 = (bf16[16,32,512]{2,1,0:T(8,128)(2,1)}, f32[32,512]{1,0:T(8,128)}, f32[32,2048]{1,0:T(8,128)}, bf16[16,32,512]{2,1,0:T(8,128)(2,1)}, bf16[2,16,32...) custom-call(bf16[32,16,512]{2,1,0:T(8,128)(2,1)} %x_hbm.1, ...), custom_call_target="tpu_custom_call" | custom-call | tf_op jit(solution)/shard_map/recurrence/pallas_call | solution.py:425
  200.5 239.5 %gradients.1 = (bf16[2,144,128,256]{3,2,1,0:T(8,128)(2,1)}, bf16[2,16,256]{2,1,0:T(8,128)(2,1)}, bf16[16,32,512]{2,1,0:T(8,128)(2,1)}) custom-call(bf16[1024,4096]{1,0:T(8,128)(2,1)} %bitcast.20, bf16[1024,1024]{1,0:T(8,128)(2,1)} %bitcast.24, bf16[1024,1024]{1,0:T(8,128)(2,1)} %bitcast.25, bf16[1024,512]{1,0:T(8,128)(2,1)} %bitcast.26, ...), custom_call_target="tpu_custom_call" | custom-call | tf_op jit(solution)/shard_map/gradients/pallas_call | solution.py:819
  440.1 22.1 %widen.1 = (bf16[32,16,512]{2,1,0:T(8,128)(2,1)}, f32[32,16,512]{2,1,0:T(8,128)}, f32[512,4,2048]{2,1,0:T(4,128)}, f32[512,4,2048]{2,1,0:T(4,128)}, f32[4,2048]{...) custom-call(bf16[2,144,128,256]{3,2,1,0:T(8,128)(2,1)} %get-tuple-element.32.res, ...), custom_call_target="tpu_custom_call" | custom-call | tf_op jit(solution)/shard_map/widen/pallas_call | solution.py:1005

commit v3 on v2

--- a/solution.py
+++ b/solution.py
@@ -11,7 +11,8 @@
 BLK = 256
 CUT = 128
 RING = 4
-LAG = 8
+LATE = 2
+RECV_RING = 32
 MESH = pl.DeviceIdType.MESH
 BF = jnp.bfloat16
 F32 = jnp.float32
@@ -61,6 +62,7 @@
     cfin_ref,
     dx_ref,
     dzg,
+    late,
     xhg,
     mg,
     drg,
@@ -88,9 +90,12 @@
     load_sem,
     ex_send,
     ex_recv,
-    y_send,
     y_recv,
-    own_sem,
+    whole_send,
+    whole_keep,
+    ring_send,
+    ring_keep,
+    late_keep,
 ):
     steps, streams, width = lay_ref.shape
     units = wp.shape[0]
@@ -199,36 +204,51 @@
             device_id_type=MESH,
         )
 
-    def pair(kind, t, away, keep, target):
+    def remote(away, target, send, recv):
+        return pltpu.make_async_remote_copy(
+            away, target, send, recv, device_id=y_dev, device_id_type=MESH
+        )
+
+    def whole(kind, src, target):
         return (
-            pltpu.make_async_remote_copy(
-                away,
-                target,
-                y_send.at[kind, t],
-                y_recv.at[kind, t],
-                device_id=y_dev,
-                device_id_type=MESH,
-            ),
-            pltpu.make_async_copy(keep, target, own_sem.at[kind, t]),
+            remote(src, target, whole_send.at[kind], y_recv.at[kind]),
+            pltpu.make_async_copy(src, target, whole_keep.at[kind]),
         )
 
     def xh_pair(t):
-        return pair(0, t, xh.at[t], xh.at[t], xhg.at[mine, place(t)])
+        return whole(0, xh.at[t], xhg.at[mine, place(t)])
+
+    def dr_pair(t):
+        return whole(1, dr.at[t], drg.at[mine, place(t)])
 
     def m_pair(t):
         slot = lax.rem(t, RING)
         away = m.at[slot, :, pl.ds(pl.multiple_of(other * half_units, half_units), half_units)]
         keep = m.at[slot, :, pl.ds(pl.multiple_of(mine * half_units, half_units), half_units)]
-        return pair(1, t, away, keep, mg.at[mine, place(t)])
-
-    def dr_pair(t):
-        return pair(2, t, dr.at[t], dr.at[t], drg.at[mine, place(t)])
+        target = mg.at[mine, place(t)]
+        return (
+            remote(away, target, ring_send.at[0, slot], y_recv.at[2]),
+            pltpu.make_async_copy(keep, target, ring_keep.at[0, slot]),
+        )
+
+    early = half_cols - LATE * BLK
 
     def dz_pair(t):
         slot = lax.rem(t, RING)
-        away = dz.at[slot, :, pl.ds(pl.multiple_of(other * half_cols, half_cols), half_cols)]
+        first = pl.multiple_of(other * half_cols, half_cols)
+        away = dz.at[slot, :, pl.ds(first, early)]
+        rest = dz.at[slot, :, pl.ds(pl.multiple_of(first + early, BLK), LATE * BLK)]
         keep = dz.at[slot, :, pl.ds(pl.multiple_of(mine * half_cols, half_cols), half_cols)]
-        return pair(3, t, away, keep, dzg.at[mine, place(t)])
+        return (
+            remote(
+                away,
+                dzg.at[mine, place(t), :, pl.ds(0, early)],
+                ring_send.at[1, slot],
+                y_recv.at[3],
+            ),
+            pltpu.make_async_copy(keep, dzg.at[mine, place(t)], ring_keep.at[1, slot]),
+            pltpu.make_async_copy(rest, late.at[place(t)], late_keep.at[slot]),
+        )
 
     def begin(copies):
         for one in copies:
@@ -236,7 +256,8 @@
 
     def sent(copies):
         copies[0].wait_send()
-        copies[1].wait()
+        for one in copies[1:]:
+            one.wait()
 
     def input_part(t):
         now = xh[t, :, :width]
@@ -404,16 +425,15 @@
 
     lax.fori_loop(0, RING, last, 0)
 
-    def finish(t, carry):
-        sent(xh_pair(t))
-        sent(dr_pair(t))
-        xh_pair(t)[0].wait_recv()
-        m_pair(t)[0].wait_recv()
-        dr_pair(t)[0].wait_recv()
-        dz_pair(t)[0].wait_recv()
-        return carry
-
-    lax.fori_loop(0, steps, finish, 0)
+    xh_all = whole(0, xh, xhg.at[mine])
+    dr_all = whole(1, dr, drg.at[mine])
+    sent(xh_all)
+    sent(dr_all)
+    xh_all[0].wait_recv()
+    dr_all[0].wait_recv()
+    remote(mg.at[mine], mg.at[mine], ring_send.at[0, 0], y_recv.at[2]).wait_recv()
+    part = dzg.at[mine, :, :, pl.ds(0, early)]
+    remote(part, part, ring_send.at[1, 0], y_recv.at[3]).wait_recv()
 
 
 def recurrence(inputs, out_grad, win, last, hidden0, cell0, bias, w_in, w_hid, proj):
@@ -430,12 +450,13 @@
             shape((streams, units), F32),
             shape((steps, streams, width), BF),
             shape((2, steps, streams, 2 * units), BF),
+            shape((steps, streams, LATE * BLK), BF),
             shape((2, steps, streams, 2 * width), BF),
             shape((2, steps, streams, units // 2), BF),
             shape((2, steps, streams, width), BF),
         ),
         in_specs=[hbm] * 2 + [vmem] * 5 + [hbm] * 3,
-        out_specs=(vmem, vmem, vmem, vmem, hbm, hbm, hbm, hbm),
+        out_specs=(vmem, vmem, vmem, vmem, hbm, hbm, hbm, hbm, hbm),
         scratch_shapes=[
             pltpu.VMEM((2, width, 4 * units), BF),
             pltpu.VMEM((4 * units, width), BF),
@@ -461,9 +482,12 @@
             pltpu.SemaphoreType.DMA((3,)),
             pltpu.SemaphoreType.DMA((2,)),
             pltpu.SemaphoreType.DMA((2,)),
-            pltpu.SemaphoreType.DMA((4, steps)),
-            pltpu.SemaphoreType.DMA((4, steps)),
-            pltpu.SemaphoreType.DMA((4, steps)),
+            pltpu.SemaphoreType.DMA((4,)),
+            pltpu.SemaphoreType.DMA((2,)),
+            pltpu.SemaphoreType.DMA((2,)),
+            pltpu.SemaphoreType.DMA((2, RING)),
+            pltpu.SemaphoreType.DMA((2, RING)),
+            pltpu.SemaphoreType.DMA((RING,)),
         ],
         compiler_params=pltpu.CompilerParams(
             collective_id=0, has_side_effects=True, vmem_limit_bytes=VMEM_LIMIT
@@ -475,6 +499,7 @@
 def gradient_kernel(
     lanes,
     dz_hbm,
+    late_hbm,
     xh_hbm,
     m_hbm,
     dr_hbm,
@@ -500,13 +525,11 @@
     red,
     load_sem,
     dz_sem,
+    late_sem,
     l_recv,
     r_recv,
-    y_recv,
-    l_send,
-    r_send,
-    y_send,
-    o_sem,
+    out_sem,
+    b_sem,
     g_send,
     g_recv,
 ):
@@ -555,17 +578,35 @@
     m_load = pltpu.make_async_copy(m_hbm, m, load_sem.at[1])
     dr_load = pltpu.make_async_copy(dr_hbm, dr, load_sem.at[2])
 
+    half_rows = rows // 2
+    my_rows = pl.ds(pl.multiple_of(mine * half_rows, half_rows), half_rows)
+    first_late = col_blocks - LATE
+    late_cols = pl.ds(first_late * BLK, LATE * BLK)
+
     def dz_load(b):
         at = pl.ds(pl.multiple_of(b * BLK, BLK), BLK)
         return pltpu.make_async_copy(dz_hbm.at[:, at], dz.at[:, at], dz_sem.at[b])
 
+    late_own = pltpu.make_async_copy(
+        dz_hbm.at[my_rows, late_cols], dz.at[my_rows, late_cols], late_sem.at[0]
+    )
+    late_far = pltpu.make_async_remote_copy(
+        late_hbm,
+        dz.at[my_rows, late_cols],
+        late_sem.at[1],
+        late_sem.at[2],
+        device_id=y_dev,
+        device_id_type=MESH,
+    )
+
     xh_load.start()
 
     def load_all(b, carry):
         dz_load(b).start()
         return carry
 
-    lax.fori_loop(0, col_blocks, load_all, 0)
+    lax.fori_loop(0, first_late, load_all, 0)
+    late_own.start()
     m_load.start()
     dr_load.start()
 
@@ -610,33 +651,36 @@
     turn(xh, xht, 0)
     peers = 4 + jnp.where(has_left, 1, 0) + jnp.where(has_right, 1, 0)
     pl.semaphore_wait(barrier, peers)
-
-    def remote(src, dst, send, recv, k, device):
+    late_far.start()
+
+    def remote(src, dst, send, recv, device):
         return pltpu.make_async_remote_copy(
-            src, dst, send.at[k], recv.at[k], device_id=device, device_id_type=MESH
+            src, dst, send, recv, device_id=device, device_id_type=MESH
         )
 
     class Chunk:
-        def __init__(self, k, own_k, left_k, right_k, res_k):
-            self.k, self.own, self.left, self.right, self.res = k, own_k, left_k, right_k, res_k
+        def __init__(self, refs, sems):
+            self.own, self.left, self.right, self.res = refs
+            self.l_recv, self.r_recv, self.l_send, self.r_send = sems[:4]
+            self.y_send, self.y_recv, self.kept = sems[4:]
 
         def to_left(self, src):
-            return remote(src, self.right, l_send, r_recv, self.k, l_dev)
+            return remote(src, self.right, self.l_send, self.r_recv, l_dev)
 
         def to_right(self, src):
-            return remote(src, self.left, r_send, l_recv, self.k, r_dev)
+            return remote(src, self.left, self.r_send, self.l_recv, r_dev)
 
         def left_in(self):
-            return remote(self.own, self.left, r_send, l_recv, self.k, l_dev)
+            return remote(self.own, self.left, self.r_send, self.l_recv, l_dev)
 
         def right_in(self):
-            return remote(self.own, self.right, l_send, r_recv, self.k, r_dev)
+            return remote(self.own, self.right, self.l_send, self.r_recv, r_dev)
 
         def to_y(self, src):
-            return remote(src, self.res, y_send, y_recv, self.k, y_dev)
+            return remote(src, self.res, self.y_send, self.y_recv, y_dev)
 
         def keep(self, src):
-            return pltpu.make_async_copy(src, self.res, o_sem.at[self.k])
+            return pltpu.make_async_copy(src, self.res, self.kept)
 
         def reduce(self, value):
             @pl.when(before)
@@ -718,13 +762,21 @@
 
             self.keep(self.own).wait()
 
+    leaving = [out_sem.at[i] for i in range(5)]
+
     def chunk(k):
-        return Chunk(k, own.at[k], from_left.at[k], from_right.at[k], res.at[mine, k])
-
-    bias = Chunk(n_all, bown, bleft, bright, bres.at[mine])
+        slot = lax.rem(k, RECV_RING)
+        refs = (own.at[k], from_left.at[k], from_right.at[k], res.at[mine, k])
+        return Chunk(refs, [l_recv.at[slot], r_recv.at[slot], *leaving])
+
+    every = Chunk((own, from_left, from_right, res.at[mine]), [l_recv.at[0], r_recv.at[0], *leaving])
+    bias = Chunk((bown, bleft, bright, bres.at[mine]), [b_sem.at[i] for i in range(7)])
     ones = jnp.ones((16, rows), BF)
     which = lax.broadcasted_iota(jnp.int32, (16, BLK), 0)
-    lag = LAG * jnp.where(before, mid - lane, lane - mid) + 3
+    far = jnp.where(before, mid - lane, lane - mid)
+    inner = jnp.logical_and(has_left, has_right)
+    lag = 5 * far + jnp.where(inner, 0, 12)
+    longest = 5 * max(mid, lanes - 1 - mid) + 12
     turns = depth // BLK
 
     def body(k, carry):
@@ -751,9 +803,17 @@
                 r = pl.multiple_of(lax.rem(k, row_blocks) * CUT, CUT)
                 at = pl.ds(pl.multiple_of(b * BLK, BLK), BLK)
 
+                @pl.when(jnp.logical_and(r == 0, b < first_late))
+                def _():
+                    dz_load(b).wait()
+
+                @pl.when(jnp.logical_and(r == 0, b == first_late))
+                def _():
+                    late_own.wait()
+                    late_far.wait_recv()
+
                 @pl.when(r == 0)
                 def _():
-                    dz_load(b).wait()
                     bsum[...] += jnp.where(which == b, mm(ones, dz[:, at]), 0.0)
 
                 acc[...] = mm(xht[pl.ds(r, CUT), :], dz[:, at])
@@ -794,20 +854,16 @@
 
         return carry
 
-    lax.fori_loop(0, n_all + LAG * max(mid, lanes - 1 - mid) + 3, body, 0)
-
-    def end(k, carry):
-        chunk(k).finish()
-        return carry
-
-    lax.fori_loop(0, n_all, end, 0)
+    lax.fori_loop(0, n_all + longest, body, 0)
+    every.finish()
+    late_far.wait_send()
     bias.finish()
     for o in (1, 2, 3):
         share(o).wait_send()
         hand_out(o).wait()
 
 
-def gradients(lanes, dzg, xhg, mg, drg, dx):
+def gradients(lanes, dzg, late, xhg, mg, drg, dx):
     rows, cols = dzg.shape
     depth = xhg.shape[1]
     n_all = (depth // CUT) * (cols // BLK) + (mg.shape[1] // CUT) * (drg.shape[1] // BLK)
@@ -815,7 +871,6 @@
     vmem = pl.BlockSpec(memory_space=pltpu.VMEM)
     hbm = pl.BlockSpec(memory_space=pl.ANY)
     shape = jax.ShapeDtypeStruct
-    sems = pltpu.SemaphoreType.DMA((n_all + 1,))
     return pl.pallas_call(
         functools.partial(gradient_kernel, lanes),
         out_shape=(
@@ -823,7 +878,7 @@
             shape((2, 16, BLK), BF),
             shape((steps, streams, width), BF),
         ),
-        in_specs=[hbm] * 4 + [vmem],
+        in_specs=[hbm] * 5 + [vmem],
         out_specs=(hbm, hbm, vmem),
         scratch_shapes=[
             pltpu.VMEM((rows, cols), BF),
@@ -844,13 +899,11 @@
             pltpu.VMEM((steps // 4, streams, width), BF),
             pltpu.SemaphoreType.DMA((3,)),
             pltpu.SemaphoreType.DMA((cols // BLK,)),
-            sems,
-            sems,
-            sems,
-            sems,
-            sems,
-            sems,
-            sems,
+            pltpu.SemaphoreType.DMA((3,)),
+            pltpu.SemaphoreType.DMA((RECV_RING,)),
+            pltpu.SemaphoreType.DMA((RECV_RING,)),
+            pltpu.SemaphoreType.DMA((5,)),
+            pltpu.SemaphoreType.DMA((7,)),
             pltpu.SemaphoreType.DMA((2, 3)),
             pltpu.SemaphoreType.DMA((2, 3)),
         ],
@@ -858,7 +911,7 @@
             collective_id=1, has_side_effects=True, vmem_limit_bytes=VMEM_LIMIT
         ),
         name="gradients",
-    )(dzg, xhg, mg, drg, dx)
+    )(dzg, late, xhg, mg, drg, dx)
 
 
 def widen_kernel(
@@ -1048,7 +1101,7 @@
     streams, steps, width = inputs.shape
     units = w_proj.shape[1]
     lanes = lax.axis_size("batch") // 2
-    lay, hfin, cfin, dx, dzg, xhg, mg, drg = recurrence(
+    lay, hfin, cfin, dx, dzg, late, xhg, mg, drg = recurrence(
         inputs,
         out_grad[0],
         win_count.reshape(1, streams),
@@ -1064,6 +1117,7 @@
     res, bres, ig = gradients(
         lanes,
         dzg.reshape(rows, 2 * units),
+        late.reshape(steps * streams, LATE * BLK),
         xhg.reshape(rows, 2 * width),
         mg.reshape(rows, units // 2),
         drg.reshape(rows, width),

time: 463 us -> 437 us (0.944)
  Pallas kernels: 461 us -> 436 us
    pallas_call x1, Pallas kernels: 240 us -> 222 us  [gradients(): pl.pallas_call(functools.partial(gradient_kernel, lanes), out_shape=(shap...]
    pallas_call x1, Pallas kernels: 200 us -> 191 us  [recurrence(): pl.pallas_call(recurrence_kernel, out_shape=(shape((steps, streams, width...]
where the time goes in v3:
time: 437 us; the launch traced here: 436 us
  Pallas kernels  436 us (100%)
    pallas_call x1, Pallas kernels, gradients(): pl.pallas_call(functools.partial(gradient_kernel, lanes), out_shape=(shap...  222 us
    pallas_call x1, Pallas kernels, recurrence(): pl.pallas_call(recurrence_kernel, out_shape=(shape((steps, streams, width...  191 us
    pallas_call x1, Pallas kernels, widen(): pl.pallas_call(functools.partial(widen_kernel, n_cat), out_shape=(shape((...  22.1 us

profile of v3, /device:TPU:0, one launch (start us, length us, event | category | flops | bytes accessed | tf_op | source)
XLA Modules:
  0.0 436.3 jit_solution(16092352659412209504)
XLA Ops:
  0.6 191.2 %recurrence.1 = (bf16[16,32,512]{2,1,0:T(8,128)(2,1)}, f32[32,512]{1,0:T(8,128)}, f32[32,2048]{1,0:T(8,128)}, bf16[16,32,512]{2,1,0:T(8,128)(2,1)}, bf16[2,16,32...) custom-call(bf16[32,16,512]{2,1,0:T(8,128)(2,1)} %x_hbm.1, ...), custom_call_target="tpu_custom_call" | custom-call | tf_op jit(solution)/shard_map/recurrence/pallas_call | solution.py:445
  191.8 222.3 %gradients.1 = (bf16[2,144,128,256]{3,2,1,0:T(8,128)(2,1)}, bf16[2,16,256]{2,1,0:T(8,128)(2,1)}, bf16[16,32,512]{2,1,0:T(8,128)(2,1)}) custom-call(bf16[1024,4096]{1,0:T(8,128)(2,1)} %bitcast.21, bf16[512,512]{1,0:T(8,128)(2,1)} %bitcast.29, bf16[1024,1024]{1,0:T(8,128)(2,1)} %bitcast.25, bf16[1024,1024]{1,0:T(8,128)(2,1)} %bitcast.26, ...), custom_call_target="tpu_custom_call" | custom-call | tf_op jit(solution)/shard_map/gradients/pallas_call | solution.py:874
  414.1 22.1 %widen.1 = (bf16[32,16,512]{2,1,0:T(8,128)(2,1)}, f32[32,16,512]{2,1,0:T(8,128)}, f32[512,4,2048]{2,1,0:T(4,128)}, f32[512,4,2048]{2,1,0:T(4,128)}, f32[4,2048]{...) custom-call(bf16[2,144,128,256]{3,2,1,0:T(8,128)(2,1)} %get-tuple-element.34.res, ...), custom_call_target="tpu_custom_call" | custom-call | tf_op jit(solution)/shard_map/widen/pallas_call | solution.py:1058

commit v4 on v3

--- a/solution.py
+++ b/solution.py
@@ -11,7 +11,7 @@
 BLK = 256
 CUT = 128
 RING = 4
-LATE = 2
+LATE = 3
 RECV_RING = 32
 MESH = pl.DeviceIdType.MESH
 BF = jnp.bfloat16
@@ -27,6 +27,11 @@
 
 def mm(a, b):
     return jnp.dot(a, b, preferred_element_type=F32)
+
+
+def mm_pad(a, b):
+    fill = jnp.zeros((128 - a.shape[0], a.shape[1]), a.dtype)
+    return mm(jnp.concatenate([a, fill], 0), b)[: a.shape[0]]
 
 
 def mm_nt(a, b):
@@ -292,7 +297,7 @@
         for j in range(tiles):
             cols = slice(j * BLK, (j + 1) * BLK)
             base = j * gate4
-            pre = z[t, :, base : base + gate4] + mm(hidden, wh[:, base : base + gate4])
+            pre = z[t, :, base : base + gate4] + mm_pad(hidden, wh[:, base : base + gate4])
             in_gate = sigmoid(pre[:, :BLK])
             forget = sigmoid(pre[:, BLK : 2 * BLK])
             cand = jnp.tanh(pre[:, 2 * BLK : 3 * BLK])
@@ -306,7 +311,7 @@
             z[t, :, base + 3 * BLK : base + gate4] = out_gate
             c[t + 1, :, cols] = jnp.where(live, new, prev)
         two = lax.rem(t, 2)
-        snd[two] = mm(m[slot], wp[...]).astype(BF)
+        snd[two] = mm_pad(m[slot], wp[...]).astype(BF)
         copy = exchange(t)
         copy.start()
         begin(xh_pair(t))
@@ -369,11 +374,11 @@
         low = (live_h * (y_low + grad_hidden) * (1.0 - squash * squash)).astype(BF)
         dr[t] = low
         live = live_of(t, BLK)
-        part = jnp.zeros((streams, width), F32)
+        grads_m = mm_pad(low, wpt[...]).astype(BF).astype(F32)
         for j in range(tiles):
             cols = slice(j * BLK, (j + 1) * BLK)
             base = j * gate4
-            grad_m = mm(low, wpt[:, cols]).astype(BF).astype(F32)
+            grad_m = grads_m[:, cols]
             in_gate = z[t, :, base : base + BLK]
             forget = z[t, :, base + BLK : base + 2 * BLK]
             cand = z[t, :, base + 2 * BLK : base + 3 * BLK]
@@ -396,7 +401,7 @@
                 grad_m * tanh_new * out_gate * (1.0 - out_gate)
             ).astype(BF)
             dc[:, cols] = (1.0 - live) * grad_c + grad_u * forget
-            part = part + mm(dz[slot, :, base : base + gate4], wht[base : base + gate4, :])
+        part = mm_pad(dz[slot], wht[...])
         snd[two] = part.astype(BF)
         copy = exchange(k)
         copy.start()

time: 437 us -> 423 us (0.968)
  Pallas kernels: 436 us -> 421 us
    pallas_call x1, Pallas kernels: 191 us -> 175 us  [recurrence(): pl.pallas_call(recurrence_kernel, out_shape=(shape((steps, streams, width...]
where the time goes in v4:
time: 423 us; the launch traced here: 422 us
  Pallas kernels  421 us (100%)
    pallas_call x1, Pallas kernels, gradients(): pl.pallas_call(functools.partial(gradient_kernel, lanes), out_shape=(shap...  224 us
    pallas_call x1, Pallas kernels, recurrence(): pl.pallas_call(recurrence_kernel, out_shape=(shape((steps, streams, width...  175 us
    pallas_call x1, Pallas kernels, widen(): pl.pallas_call(functools.partial(widen_kernel, n_cat), out_shape=(shape((...  22.1 us

profile of v4, /device:TPU:0, one launch (start us, length us, event | category | flops | bytes accessed | tf_op | source)
XLA Modules:
  0.0 422.0 jit_solution(12728737818887099865)
XLA Ops:
  0.6 175.1 %recurrence.1 = (bf16[16,32,512]{2,1,0:T(8,128)(2,1)}, f32[32,512]{1,0:T(8,128)}, f32[32,2048]{1,0:T(8,128)}, bf16[16,32,512]{2,1,0:T(8,128)(2,1)}, bf16[2,16,32...) custom-call(bf16[32,16,512]{2,1,0:T(8,128)(2,1)} %x_hbm.1, ...), custom_call_target="tpu_custom_call" | custom-call | tf_op jit(solution)/shard_map/recurrence/pallas_call | solution.py:450
  175.7 224.2 %gradients.1 = (bf16[2,144,128,256]{3,2,1,0:T(8,128)(2,1)}, bf16[2,16,256]{2,1,0:T(8,128)(2,1)}, bf16[16,32,512]{2,1,0:T(8,128)(2,1)}) custom-call(bf16[1024,4096]{1,0:T(8,128)(2,1)} %bitcast.21, bf16[512,768]{1,0:T(8,128)(2,1)} %bitcast.28, bf16[1024,1024]{1,0:T(8,128)(2,1)} %bitcast.25, bf16[1024,1024]{1,0:T(8,128)(2,1)} %bitcast.26, ...), custom_call_target="tpu_custom_call" | custom-call | tf_op jit(solution)/shard_map/gradients/pallas_call | solution.py:879
  399.9 22.1 %widen.1 = (bf16[32,16,512]{2,1,0:T(8,128)(2,1)}, f32[32,16,512]{2,1,0:T(8,128)}, f32[512,4,2048]{2,1,0:T(4,128)}, f32[512,4,2048]{2,1,0:T(4,128)}, f32[4,2048]{...) custom-call(bf16[2,144,128,256]{3,2,1,0:T(8,128)(2,1)} %get-tuple-element.34.res, ...), custom_call_target="tpu_custom_call" | custom-call | tf_op jit(solution)/shard_map/widen/pallas_call | solution.py:1063

commit v5 on v4

--- a/solution.py
+++ b/solution.py
@@ -75,7 +75,6 @@
     wht,
     wp,
     wpt,
-    raw,
     z,
     c,
     th,
@@ -120,19 +119,16 @@
     def place(t):
         return t + flip * (steps - 1 - 2 * t)
 
-    slots = raw.shape[0]
-    span = raw.shape[2]
-    halves = units // span
-    blocks = halves * width * 4 // BLK
-
-    def fetch(n, w_hbm, slot):
-        b = lax.div(n, halves)
-        col = lax.rem(n, halves)
+    slots = wpt.shape[0] // BLK
+    blocks = width * 4 // BLK
+
+    def raw(slot):
+        return wpt.at[pl.ds(pl.multiple_of(slot * BLK, BLK), BLK)]
+
+    def fetch(b, w_hbm, slot):
         return pltpu.make_async_copy(
-            w_hbm.reshape(width * 4, units).at[
-                pl.ds(pl.multiple_of(b * BLK, BLK), BLK), pl.ds(pl.multiple_of(col * span, span), span)
-            ],
-            raw.at[slot],
+            w_hbm.reshape(width * 4, units).at[pl.ds(pl.multiple_of(b * BLK, BLK), BLK)],
+            raw(slot),
             raw_sem.at[slot],
         )
 
@@ -167,16 +163,12 @@
         fetch(0, wx_hbm, slot).wait()
         which = lax.div(n, blocks)
         left = n - which * blocks
-        row = pl.multiple_of(lax.div(left, halves) * 64, 64)
-        col = lax.rem(left, halves) * (4 * span)
-        for j in range(span // BLK):
-            got = mm(order, raw[slot, :, j * BLK : (j + 1) * BLK]).astype(BF)
+        row = pl.multiple_of(left * 64, 64)
+        for j in range(tiles):
+            got = mm(order, raw(slot)[:, j * BLK : (j + 1) * BLK]).astype(BF)
             for g in range(4):
-                w[
-                    which,
-                    pl.ds(row, 64),
-                    pl.ds(pl.multiple_of(col + j * gate4 + g * BLK, BLK), BLK),
-                ] = got[g * 64 : (g + 1) * 64]
+                base = j * gate4 + g * BLK
+                w[which, pl.ds(row, 64), base : base + BLK] = got[g * 64 : (g + 1) * 64]
         return carry
 
     lax.fori_loop(0, 2 * blocks, spread, 0)
@@ -374,7 +366,7 @@
         low = (live_h * (y_low + grad_hidden) * (1.0 - squash * squash)).astype(BF)
         dr[t] = low
         live = live_of(t, BLK)
-        grads_m = mm_pad(low, wpt[...]).astype(BF).astype(F32)
+        grads_m = mm_pad(low, wpt[:width, :]).astype(BF).astype(F32)
         for j in range(tiles):
             cols = slice(j * BLK, (j + 1) * BLK)
             base = j * gate4
@@ -466,8 +458,7 @@
             pltpu.VMEM((2, width, 4 * units), BF),
             pltpu.VMEM((4 * units, width), BF),
             pltpu.VMEM((units, width), BF),
-            pltpu.VMEM((width, units), BF),
-            pltpu.VMEM((4, BLK, units // 2), BF),
+            pltpu.VMEM((max(width, 4 * BLK), units), BF),
             pltpu.VMEM((steps, streams, 4 * units), F32),
             pltpu.VMEM((steps + 1, streams, units), F32),
             pltpu.VMEM((steps, streams, width), F32),
@@ -937,17 +928,25 @@
     cfin_out,
     low,
     wide,
+    lay_low,
     lay_buf,
+    ig_low,
     ig_buf,
     p_low,
+    p_wide,
+    b_wide,
+    h_buf,
+    c_buf,
     in_sem,
     out_sem,
     p_sem,
-    s_sem,
+    s_in,
+    s_out,
     ig_sem,
+    wp_sem,
 ):
     width, _, units = wx_out.shape
-    steps, streams, _ = lay_in.shape
+    steps, streams, _ = lay_low.shape
     slots = low.shape[0]
     row_blocks = low.shape[1]
     half = row_blocks // 2
@@ -985,11 +984,24 @@
         pltpu.make_async_copy(res.at[o, pl.ds(n_cat, n_proj)], p_low.at[o], p_sem.at[o])
         for o in range(2)
     ]
-    states = [
-        pltpu.make_async_copy(hfin_in, hfin_out, s_sem.at[0]),
-        pltpu.make_async_copy(cfin_in, cfin_out, s_sem.at[1]),
+    taken = [
+        pltpu.make_async_copy(src, dst, s_in.at[i])
+        for i, (src, dst) in enumerate(
+            ((lay_in, lay_low), (ig_in, ig_low), (hfin_in, h_buf), (cfin_in, c_buf))
+        )
     ]
-    for one in proj + states:
+    given = [
+        pltpu.make_async_copy(src, dst, s_out.at[i])
+        for i, (src, dst) in enumerate(
+            (
+                (lay_buf, lay_out.reshape(streams * steps, width)),
+                (h_buf, hfin_out),
+                (c_buf, cfin_out),
+                (b_wide, b_out),
+            )
+        )
+    ]
+    for one in taken + proj:
         one.start()
 
     def body(k, carry):
@@ -1012,41 +1024,74 @@
 
         return carry
 
-    lax.fori_loop(0, slots, body, 0)
-
-    t = lax.broadcasted_iota(jnp.int32, (steps, streams * steps), 0)
-    r = lax.broadcasted_iota(jnp.int32, (steps, streams * steps), 1)
-    flat = lay_in[...].reshape(streams * steps, width)
-    bunch = BLK // steps
-    for b in range(streams // bunch):
-        want = jnp.concatenate(
-            [jnp.where(r == t * streams + b * bunch + s, 1.0, 0.0) for s in range(bunch)], 0
-        ).astype(BF)
-        lay_buf[b * BLK : (b + 1) * BLK, :] = mm(want, flat).astype(BF)
-    lay_copy = pltpu.make_async_copy(lay_buf, lay_out.reshape(streams * steps, width), s_sem.at[2])
-    lay_copy.start()
-    ig_copies = []
-    for step in range(steps):
-        ig_buf[step] = ig_in[step].astype(F32)
-        ig_copies.append(
-            pltpu.make_async_copy(ig_buf.at[step], ig_out.at[:, step, :], ig_sem.at[step])
+    def layer_rows():
+        taken[0].wait()
+        t = lax.broadcasted_iota(jnp.int32, (steps, streams * steps), 0)
+        r = lax.broadcasted_iota(jnp.int32, (steps, streams * steps), 1)
+        flat = lay_low[...].reshape(streams * steps, width)
+        bunch = BLK // steps
+        for b in range(streams // bunch):
+            want = jnp.concatenate(
+                [jnp.where(r == t * streams + b * bunch + s, 1.0, 0.0) for s in range(bunch)], 0
+            ).astype(BF)
+            lay_buf[b * BLK : (b + 1) * BLK, :] = mm(want, flat).astype(BF)
+        given[0].start()
+
+    def states():
+        for i in (2, 3):
+            taken[i].wait()
+            given[i - 1].start()
+
+    def input_rows():
+        taken[1].wait()
+        for step in range(steps):
+            ig_buf[step] = ig_low[step].astype(F32)
+            ig_copy(step).start()
+
+    def ig_copy(step):
+        return pltpu.make_async_copy(ig_buf.at[step], ig_out.at[:, step, :], ig_sem.at[step])
+
+    def bias_rows():
+        for owner in range(2):
+            for b in range(col_blocks):
+                u = owner * (units // 2) + (b // 4) * BLK
+                b_wide[b % 4 : b % 4 + 1, u : u + BLK] = bres[owner, b : b + 1, :].astype(F32)
+        given[3].start()
+
+    proj_rows = n_proj // proj_cols * CUT
+
+    def proj_copy(owner):
+        return pltpu.make_async_copy(
+            p_wide.at[owner], wp_out.at[pl.ds(owner * proj_rows, proj_rows)], wp_sem.at[owner]
         )
-        ig_copies[-1].start()
-    for owner in range(2):
+
+    def proj_part(owner):
         proj[owner].wait()
         for n in range(n_proj):
-            row = owner * (units // 2) + (n // proj_cols) * CUT
+            row = (n // proj_cols) * CUT
             col = (n % proj_cols) * BLK
-            wp_out[row : row + CUT, col : col + BLK] = p_low[owner, n].astype(F32)
-        for b in range(col_blocks):
-            u = owner * (units // 2) + (b // 4) * BLK
-            b_out[b % 4 : b % 4 + 1, u : u + BLK] = bres[owner, b : b + 1, :].astype(F32)
-
-    lax.fori_loop(slots, count, body, 0)
+            p_wide[owner, row : row + CUT, col : col + BLK] = p_low[owner, n].astype(F32)
+        proj_copy(owner).start()
+
+    extras = [
+        layer_rows,
+        states,
+        input_rows,
+        bias_rows,
+        functools.partial(proj_part, 0),
+        functools.partial(proj_part, 1),
+    ]
+    at = slots
+    lax.fori_loop(0, at, body, 0)
+    for extra in extras:
+        extra()
+        lax.fori_loop(at, at + 3, body, 0)
+        at += 3
+    lax.fori_loop(at, count, body, 0)
     for k in range(count - slots, count):
         for one in store(k):
             one.wait()
-    for one in [*states, lay_copy, *ig_copies]:
+    for one in [*given, *(ig_copy(step) for step in range(steps)), proj_copy(0), proj_copy(1)]:
         one.wait()
 
 
@@ -1056,7 +1101,7 @@
     row_blocks = 2 * width // CUT
     n_cat = row_blocks * (2 * units // BLK)
     n_proj = res.shape[1] - n_cat
-    slots = 4
+    slots = 6
     vmem = pl.BlockSpec(memory_space=pltpu.VMEM)
     hbm = pl.BlockSpec(memory_space=pl.ANY)
     shape = jax.ShapeDtypeStruct
@@ -1072,19 +1117,27 @@
             shape((streams, width), F32),
             shape((streams, units), F32),
         ),
-        in_specs=[hbm, vmem, vmem, vmem, hbm, hbm],
-        out_specs=(hbm, hbm, hbm, hbm, vmem, vmem, hbm, hbm),
+        in_specs=[hbm, vmem, hbm, hbm, hbm, hbm],
+        out_specs=(hbm,) * 8,
         scratch_shapes=[
             pltpu.VMEM((slots, row_blocks, CUT, BLK), BF),
             pltpu.VMEM((slots, 2, width, BLK), F32),
+            pltpu.VMEM((steps, streams, width), BF),
             pltpu.VMEM((streams * steps, width), BF),
+            pltpu.VMEM((steps, streams, width), BF),
             pltpu.VMEM((steps, streams, width), F32),
             pltpu.VMEM((2, n_proj, CUT, BLK), BF),
+            pltpu.VMEM((2, units // 2, width), F32),
+            pltpu.VMEM((4, units), F32),
+            pltpu.VMEM((streams, width), F32),
+            pltpu.VMEM((streams, units), F32),
             pltpu.SemaphoreType.DMA((slots,)),
             pltpu.SemaphoreType.DMA((slots, 2)),
             pltpu.SemaphoreType.DMA((2,)),
-            pltpu.SemaphoreType.DMA((3,)),
+            pltpu.SemaphoreType.DMA((4,)),
+            pltpu.SemaphoreType.DMA((4,)),
             pltpu.SemaphoreType.DMA((steps,)),
+            pltpu.SemaphoreType.DMA((2,)),
         ],
         compiler_params=pltpu.CompilerParams(vmem_limit_bytes=VMEM_LIMIT),
         name="widen",

time: 423 us -> 417 us (0.986)
  Pallas kernels: 421 us -> 416 us
where the time goes in v5:
time: 417 us
  Pallas kernels  416 us (100%)
    pallas_call x1, Pallas kernels, gradients(): pl.pallas_call(functools.partial(gradient_kernel, lanes), out_shape=(shap...  224 us
    pallas_call x1, Pallas kernels, recurrence(): pl.pallas_call(recurrence_kernel, out_shape=(shape((steps, streams, width...  171 us
    pallas_call x1, Pallas kernels, widen(): pl.pallas_call(functools.partial(widen_kernel, n_cat), out_shape=(shape((...  20.8 us

profile of v5, /device:TPU:0, one launch (start us, length us, event | category | flops | bytes accessed | tf_op | source)
XLA Modules:
  0.0 416.5 jit_solution(6688975296400266717)
XLA Ops:
  0.6 170.9 %recurrence.1 = (bf16[16,32,512]{2,1,0:T(8,128)(2,1)}, f32[32,512]{1,0:T(8,128)}, f32[32,2048]{1,0:T(8,128)}, bf16[16,32,512]{2,1,0:T(8,128)(2,1)}, bf16[2,16,32...) custom-call(bf16[32,16,512]{2,1,0:T(8,128)(2,1)} %x_hbm.1, ...), custom_call_target="tpu_custom_call" | custom-call | tf_op jit(solution)/shard_map/recurrence/pallas_call | solution.py:442
  171.6 224.2 %gradients.1 = (bf16[2,144,128,256]{3,2,1,0:T(8,128)(2,1)}, bf16[2,16,256]{2,1,0:T(8,128)(2,1)}, bf16[16,32,512]{2,1,0:T(8,128)(2,1)}) custom-call(bf16[1024,4096]{1,0:T(8,128)(2,1)} %bitcast.21, bf16[512,768]{1,0:T(8,128)(2,1)} %bitcast.28, bf16[1024,1024]{1,0:T(8,128)(2,1)} %bitcast.25, bf16[1024,1024]{1,0:T(8,128)(2,1)} %bitcast.26, ...), custom_call_target="tpu_custom_call" | custom-call | tf_op jit(solution)/shard_map/gradients/pallas_call | solution.py:870
  395.7 20.8 %widen.1 = (bf16[32,16,512]{2,1,0:T(8,128)(2,1)}, f32[32,16,512]{2,1,0:T(8,128)}, f32[512,4,2048]{2,1,0:T(4,128)}, f32[512,4,2048]{2,1,0:T(4,128)}, f32[4,2048]{...) custom-call(bf16[2,144,128,256]{3,2,1,0:T(8,128)(2,1)} %get-tuple-element.34.res, ...), custom_call_target="tpu_custom_call" | custom-call | tf_op jit(solution)/shard_map/widen/pallas_call | solution.py:1108

commit v6 on v5

--- a/solution.py
+++ b/solution.py
@@ -54,18 +54,18 @@
 def recurrence_kernel(
     x_hbm,
     y_hbm,
-    win_ref,
-    last_ref,
-    h0_ref,
-    c0_ref,
-    bias_ref,
+    win_hbm,
+    last_hbm,
+    h0_hbm,
+    c0_hbm,
+    bias_hbm,
     wx_hbm,
     wh_hbm,
     wp_hbm,
-    lay_ref,
-    hfin_ref,
-    cfin_ref,
-    dx_ref,
+    lay_hbm,
+    hfin_hbm,
+    cfin_hbm,
+    dx_hbm,
     dzg,
     late,
     xhg,
@@ -90,8 +90,15 @@
     lens,
     snd,
     rcv,
+    win_ref,
+    last_ref,
+    h0_ref,
+    bias_ref,
+    lay_ref,
+    dx_ref,
     raw_sem,
     load_sem,
+    state_sem,
     ex_send,
     ex_recv,
     y_recv,
@@ -101,7 +108,7 @@
     ring_keep,
     late_keep,
 ):
-    steps, streams, width = lay_ref.shape
+    steps, streams, width = lay_hbm.shape
     units = wp.shape[0]
     tiles = units // BLK
     gate4 = 4 * BLK
@@ -148,9 +155,29 @@
     x_copy = pltpu.make_async_copy(x_hbm.reshape(streams * steps, width), x_flat, load_sem.at[0])
     y_copy = pltpu.make_async_copy(y_hbm.reshape(streams * steps, width), y_flat, load_sem.at[1])
     proj_copy = pltpu.make_async_copy(wp_hbm, wp, load_sem.at[2])
-    x_copy.start()
-    proj_copy.start()
-    y_copy.start()
+    small = [
+        pltpu.make_async_copy(src, dst, load_sem.at[3 + i])
+        for i, (src, dst) in enumerate(
+            (
+                (win_hbm, win_ref),
+                (last_hbm, last_ref),
+                (h0_hbm, h0_ref),
+                (bias_hbm, bias_ref),
+                (c0_hbm, c.at[0]),
+            )
+        )
+    ]
+    finals = [
+        pltpu.make_async_copy(lay_ref, lay_hbm, state_sem.at[0]),
+        pltpu.make_async_copy(h0_ref, hfin_hbm, state_sem.at[1]),
+        pltpu.make_async_copy(c.at[steps], cfin_hbm, state_sem.at[2]),
+    ]
+
+    def dx_copy(t):
+        return pltpu.make_async_copy(dx_ref.at[t], dx_hbm.at[t], state_sem.at[3])
+
+    for one in [x_copy, proj_copy, y_copy, *small]:
+        one.start()
     barrier = pltpu.get_barrier_semaphore()
     pl.semaphore_signal(barrier, 1, device_id=x_dev, device_id_type=MESH)
     pl.semaphore_signal(barrier, 1, device_id=y_dev, device_id_type=MESH)
@@ -174,6 +201,8 @@
     lax.fori_loop(0, 2 * blocks, spread, 0)
     wx, wh = w.at[0], w.at[1]
 
+    for one in small:
+        one.wait()
     row_len = ((win_ref[...] - 1) * WIN + last_ref[...]).astype(F32)
     rows = lax.broadcasted_iota(jnp.int32, (streams, streams), 0)
     cols = lax.broadcasted_iota(jnp.int32, (streams, streams), 1)
@@ -269,7 +298,6 @@
     x_copy.wait()
     xh[0, :, :width] = pick(x_flat, 0)
     xh[0, :, hid] = h0_ref[...].astype(BF)
-    c[0] = c0_ref[...]
     input_part(0)
     proj_copy.wait()
     y_copy.wait()
@@ -340,12 +368,13 @@
 
         @pl.when(t + 1 == steps)
         def _():
-            hfin_ref[...] = after
+            h0_ref[...] = after
 
         return carry
 
     lax.fori_loop(0, steps, forward, 0)
-    cfin_ref[...] = c[steps]
+    for one in finals:
+        one.start()
     dc[...] = jnp.zeros_like(dc)
     dh[...] = jnp.zeros_like(dh)
     y_now[0] = pick(y_flat, steps - 1)
@@ -409,6 +438,7 @@
             base = j * gate4
             grad_x = grad_x + mm_nt(dz[slot, :, base : base + gate4], wx[:, base : base + gate4])
         dx_ref[place(t)] = grad_x.astype(BF)
+        dx_copy(place(t)).start()
         copy.wait()
         dh[...] = (1.0 - live_h) * grad_hidden + (snd[two].astype(F32) + rcv[two].astype(F32))
         return carry
@@ -422,6 +452,9 @@
 
     lax.fori_loop(0, RING, last, 0)
 
+    for one in finals:
+        one.wait()
+    pltpu.make_async_copy(dx_ref, dx_hbm, state_sem.at[3]).wait()
     xh_all = whole(0, xh, xhg.at[mine])
     dr_all = whole(1, dr, drg.at[mine])
     sent(xh_all)
@@ -436,7 +469,6 @@
 def recurrence(inputs, out_grad, win, last, hidden0, cell0, bias, w_in, w_hid, proj):
     streams, steps, width = inputs.shape
     units = proj.shape[0]
-    vmem = pl.BlockSpec(memory_space=pltpu.VMEM)
     hbm = pl.BlockSpec(memory_space=pl.ANY)
     shape = jax.ShapeDtypeStruct
     return pl.pallas_call(
@@ -452,8 +484,8 @@
             shape((2, steps, streams, units // 2), BF),
             shape((2, steps, streams, width), BF),
         ),
-        in_specs=[hbm] * 2 + [vmem] * 5 + [hbm] * 3,
-        out_specs=(vmem, vmem, vmem, vmem, hbm, hbm, hbm, hbm, hbm),
+        in_specs=[hbm] * 10,
+        out_specs=(hbm,) * 9,
         scratch_shapes=[
             pltpu.VMEM((2, width, 4 * units), BF),
             pltpu.VMEM((4 * units, width), BF),
@@ -474,8 +506,15 @@
             pltpu.VMEM((streams, 128), F32),
             pltpu.VMEM((2, streams, width), BF),
             pltpu.VMEM((2, streams, width), BF),
+            pltpu.VMEM((1, streams), jnp.int32),
+            pltpu.VMEM((1, streams), jnp.int32),
+            pltpu.VMEM((streams, width), F32),
+            pltpu.VMEM((4, units), F32),
+            pltpu.VMEM((steps, streams, width), BF),
+            pltpu.VMEM((steps, streams, width), BF),
             pltpu.SemaphoreType.DMA((4,)),
-            pltpu.SemaphoreType.DMA((3,)),
+            pltpu.SemaphoreType.DMA((8,)),
+            pltpu.SemaphoreType.DMA((4,)),
             pltpu.SemaphoreType.DMA((2,)),
             pltpu.SemaphoreType.DMA((2,)),
             pltpu.SemaphoreType.DMA((4,)),
@@ -499,10 +538,10 @@
     xh_hbm,
     m_hbm,
     dr_hbm,
-    dx_ref,
+    dx_hbm,
     res,
     bres,
-    ig_ref,
+    ig_hbm,
     dz,
     xh,
     xht,
@@ -520,6 +559,7 @@
     rx,
     red,
     load_sem,
+    xh_sem,
     dz_sem,
     late_sem,
     l_recv,
@@ -570,7 +610,10 @@
     def _():
         pl.semaphore_signal(barrier, 1, device_id=r_dev, device_id_type=MESH)
 
-    xh_load = pltpu.make_async_copy(xh_hbm, xh, load_sem.at[0])
+    def xh_load(a):
+        at = pl.ds(pl.multiple_of(a * BLK, BLK), BLK)
+        return pltpu.make_async_copy(xh_hbm.at[:, at], xh.at[:, at], xh_sem.at[a])
+
     m_load = pltpu.make_async_copy(m_hbm, m, load_sem.at[1])
     dr_load = pltpu.make_async_copy(dr_hbm, dr, load_sem.at[2])
 
@@ -595,13 +638,16 @@
         device_id_type=MESH,
     )
 
-    xh_load.start()
-
     def load_all(b, carry):
         dz_load(b).start()
         return carry
 
-    lax.fori_loop(0, first_late, load_all, 0)
+    turns = depth // BLK
+    xh_load(0).start()
+    dz_load(0).start()
+    for a in range(1, turns):
+        xh_load(a).start()
+    lax.fori_loop(1, first_late, load_all, 0)
     late_own.start()
     m_load.start()
     dr_load.start()
@@ -615,16 +661,23 @@
                 eye, src[b * BLK : (b + 1) * BLK, at]
             ).astype(BF)
 
-    quarter = dx_ref.shape[0] // 4
+    quarter = dx_hbm.shape[0] // 4
     me = flip + 2 * unit
 
     def member(o):
         p = group(o)
         return p["dir"] + 2 * p["unit"]
 
+    dx_own = pltpu.make_async_copy(
+        dx_hbm.at[pl.ds(me * quarter, quarter)], red.at[0], load_sem.at[0]
+    )
+    ig_own = pltpu.make_async_copy(
+        red.at[1], ig_hbm.at[pl.ds(me * quarter, quarter)], load_sem.at[0]
+    )
+
     def share(o):
         return pltpu.make_async_remote_copy(
-            dx_ref.at[pl.ds(member(o) * quarter, quarter)],
+            dx_hbm.at[pl.ds(member(o) * quarter, quarter)],
             rx.at[o - 1],
             g_send.at[0, o - 1],
             g_recv.at[0, o - 1],
@@ -634,20 +687,20 @@
 
     def hand_out(o):
         return pltpu.make_async_remote_copy(
-            red,
-            ig_ref.at[pl.ds(me * quarter, quarter)],
+            red.at[1],
+            ig_hbm.at[pl.ds(me * quarter, quarter)],
             g_send.at[1, o - 1],
             g_recv.at[1, o - 1],
             device_id=group(o),
             device_id_type=MESH,
         )
 
-    bsum[...] = jnp.zeros_like(bsum)
-    xh_load.wait()
-    turn(xh, xht, 0)
     peers = 4 + jnp.where(has_left, 1, 0) + jnp.where(has_right, 1, 0)
     pl.semaphore_wait(barrier, peers)
     late_far.start()
+    bsum[...] = jnp.zeros_like(bsum)
+    xh_load(0).wait()
+    turn(xh, xht, 0)
 
     def remote(src, dst, send, recv, device):
         return pltpu.make_async_remote_copy(
@@ -773,17 +826,18 @@
     inner = jnp.logical_and(has_left, has_right)
     lag = 5 * far + jnp.where(inner, 0, 12)
     longest = 5 * max(mid, lanes - 1 - mid) + 12
-    turns = depth // BLK
 
     def body(k, carry):
         @pl.when(jnp.logical_and(k > 0, k < turns))
         def _():
+            xh_load(k).wait()
             turn(xh, xht, k)
 
         @pl.when(k == row_blocks)
         def _():
             m_load.wait()
             dr_load.wait()
+            dx_own.start()
             for o in (1, 2, 3):
                 share(o).start()
 
@@ -829,12 +883,13 @@
 
         @pl.when(k == 4 * row_blocks)
         def _():
-            sums = dx_ref[pl.ds(me * quarter, quarter)].astype(F32)
+            dx_own.wait()
+            sums = red[0].astype(F32)
             for o in (1, 2, 3):
                 share(o).wait_recv()
                 sums = sums + rx[o - 1].astype(F32)
-            red[...] = sums.astype(BF)
-            ig_ref[pl.ds(me * quarter, quarter)] = red[...]
+            red[1] = sums.astype(BF)
+            ig_own.start()
             for o in (1, 2, 3):
                 hand_out(o).start()
 
@@ -853,6 +908,7 @@
     lax.fori_loop(0, n_all + longest, body, 0)
     every.finish()
     late_far.wait_send()
+    ig_own.wait()
     bias.finish()
     for o in (1, 2, 3):
         share(o).wait_send()
@@ -864,7 +920,6 @@
     depth = xhg.shape[1]
     n_all = (depth // CUT) * (cols // BLK) + (mg.shape[1] // CUT) * (drg.shape[1] // BLK)
     steps, streams, width = dx.shape
-    vmem = pl.BlockSpec(memory_space=pltpu.VMEM)
     hbm = pl.BlockSpec(memory_space=pl.ANY)
     shape = jax.ShapeDtypeStruct
     return pl.pallas_call(
@@ -874,8 +929,8 @@
             shape((2, 16, BLK), BF),
             shape((steps, streams, width), BF),
         ),
-        in_specs=[hbm] * 5 + [vmem],
-        out_specs=(hbm, hbm, vmem),
+        in_specs=[hbm] * 6,
+        out_specs=(hbm, hbm, hbm),
         scratch_shapes=[
             pltpu.VMEM((rows, cols), BF),
             pltpu.VMEM((rows, depth), BF),
@@ -892,8 +947,9 @@
             pltpu.VMEM((16, BLK), BF),
             pltpu.VMEM((16, BLK), BF),
             pltpu.VMEM((3, steps // 4, streams, width), BF),
-            pltpu.VMEM((steps // 4, streams, width), BF),
+            pltpu.VMEM((2, steps // 4, streams, width), BF),
             pltpu.SemaphoreType.DMA((3,)),
+            pltpu.SemaphoreType.DMA((depth // BLK,)),
             pltpu.SemaphoreType.DMA((cols // BLK,)),
             pltpu.SemaphoreType.DMA((3,)),
             pltpu.SemaphoreType.DMA((RECV_RING,)),

time: 417 us -> 413 us (level)
  no operation moved by 1% of the time
where the time goes in v6:
time: 413 us
  Pallas kernels  412 us (100%)
    pallas_call x1, Pallas kernels, gradients(): pl.pallas_call(functools.partial(gradient_kernel, lanes), out_shape=(shap...  222 us
    pallas_call x1, Pallas kernels, recurrence(): pl.pallas_call(recurrence_kernel, out_shape=(shape((steps, streams, width...  169 us
    pallas_call x1, Pallas kernels, widen(): pl.pallas_call(functools.partial(widen_kernel, n_cat), out_shape=(shape((...  20.8 us

profile of v6, /device:TPU:0, one launch (start us, length us, event | category | flops | bytes accessed | tf_op | source)
XLA Modules:
  0.0 412.9 jit_solution(9210919697440562009)
XLA Ops:
  0.6 169.0 %recurrence.1 = (bf16[16,32,512]{2,1,0:T(8,128)(2,1)}, f32[32,512]{1,0:T(8,128)}, f32[32,2048]{1,0:T(8,128)}, bf16[16,32,512]{2,1,0:T(8,128)(2,1)}, bf16[2,16,32...) custom-call(bf16[32,16,512]{2,1,0:T(8,128)(2,1)} %x_hbm.1, ...), custom_call_target="tpu_custom_call" | custom-call | tf_op jit(solution)/shard_map/recurrence/pallas_call | solution.py:474
  169.7 222.4 %gradients.1 = (bf16[2,144,128,256]{3,2,1,0:T(8,128)(2,1)}, bf16[2,16,256]{2,1,0:T(8,128)(2,1)}, bf16[16,32,512]{2,1,0:T(8,128)(2,1)}) custom-call(bf16[1024,4096]{1,0:T(8,128)(2,1)} %bitcast.21, bf16[512,768]{1,0:T(8,128)(2,1)} %bitcast.28, bf16[1024,1024]{1,0:T(8,128)(2,1)} %bitcast.25, bf16[1024,1024]{1,0:T(8,128)(2,1)} %bitcast.26, ...), custom_call_target="tpu_custom_call" | custom-call | tf_op jit(solution)/shard_map/gradients/pallas_call | solution.py:925
  392.1 20.8 %widen.1 = (bf16[32,16,512]{2,1,0:T(8,128)(2,1)}, f32[32,16,512]{2,1,0:T(8,128)}, f32[512,4,2048]{2,1,0:T(4,128)}, f32[512,4,2048]{2,1,0:T(4,128)}, f32[4,2048]{...) custom-call(bf16[2,144,128,256]{3,2,1,0:T(8,128)(2,1)} %get-tuple-element.34.res, ...), custom_call_target="tpu_custom_call" | custom-call | tf_op jit(solution)/shard_map/widen/pallas_call | solution.py:1164
